TPU v7x, 32 devices: a whole 2x2x4 slice. The times are simulated.
32 devices in a mesh: req: 16 (over z, y, x), ctx: 2 (over core).
Axes of the slice: x: 2, y: 2, z: 4, core: 2. Of those that a mesh axis runs over, the one named last changes fastest.
Arguments:
- conv_input: bfloat16 [16, 512, 10240], P('req', 'ctx'), may hold values from -6 to 6
- gate_input: bfloat16 [16, 512, 8192], P('req', 'ctx'), may hold values from -6 to 6
- dt_raw: bfloat16 [16, 512, 128], P('req', 'ctx'), may hold values from -3 to 3
- conv_weight: float32 [4, 10240], replicated, may hold values from -3 to 3
- conv_bias: float32 [10240], replicated, may hold values from -3 to 3
- dt_bias: float32 [128], replicated
- a_log: float32 [128], replicated
- d_skip: float32 [128], replicated, may hold values from 0.5 to 2
- norm_weight: float32 [8192], replicated, may hold values from 0.5 to 1.5
- conv_cache: bfloat16 [16, 3, 10240], P('req'), may hold values from -6 to 6
- state_pool: float32 [1024, 256, 128], P(('req', 'ctx')), may hold values from -6 to 6
- page_owner: int32 [16, 32], replicated, may hold values from 0 to 31, as said below
- page_slot: int32 [16, 32], replicated, may hold values from 0 to 31, as said below
- prefix_len: int32 [16], replicated, may hold values from 0 to 32767, as said below
- new_count: int32 [16], replicated, may hold values from 64 to 512, as said below
Outputs:
- mixed: bfloat16 [16, 512, 8192], P('req', 'ctx')
- new_conv: bfloat16 [16, 3, 10240], P('req')
- new_pool: float32 [1024, 256, 128], P(('req', 'ctx'))
Inputs may be any that keep to these rules, and one draw needn't show every extreme that they name: `page_owner`: page j of request r holds rows j * 256 to (j + 1) * 256 - 1 of its state; devices are counted as req index times the ctx axis's size plus ctx index. The 16 pages j of one request with the same j // 16 lie on different devices, and every device holds exactly 16 pages of all requests together. `page_slot`: the pages held by one device lie in different slots; other slots hold nothing of these requests. `prefix_len`: some request has prefix length 0 in every draw. `new_count`: both ends are reached in every draw; the new tokens of a request fill its first slots.
All inputs are finite; a program needn't handle non-finite values.
Results may differ from a plain program's by a relative error of at most 0.0095.
Values may be sent and summed in bfloat16 or wider, within the bound.
A program may use at most 192 MiB of HBM per device.

v0:
```python
import jax
import jax.numpy as jnp
from jax import lax
from jax.sharding import PartitionSpec as P

GROUPS = 8


def passed_along(value, axis, steps):
    count = lax.axis_size(axis)
    first, last = (max(0, -steps), min(count, count - steps))
    return lax.ppermute(value, axis, [(source, source + steps) for source in range(first, last)])


def prefix_2(x, axis, combine, identity):
    count, mine = (lax.axis_size(axis), lax.axis_index(axis))
    everything = jax.tree.map(lambda part: lax.all_gather(part, axis), x)
    start = jax.tree.map(
        lambda part, zero: jnp.broadcast_to(jnp.asarray(zero, part.dtype), part.shape), x, identity
    )

    def step(k, before):
        reached = k < mine
        new = combine(before, jax.tree.map(lambda part: part[k], everything))
        return jax.tree.map(lambda a, b: jnp.where(reached, a, b), new, before)

    return lax.fori_loop(0, count, step, start)


def conv_silu(extended, conv_weight, conv_bias, count_rows):
    accum = jnp.broadcast_to(conv_bias, (count_rows, conv_bias.shape[0]))
    for tap in range(conv_weight.shape[0]):
        accum = accum + conv_weight[tap] * extended[tap : tap + count_rows].astype(jnp.float32)
    return jax.nn.silu(accum).astype(jnp.bfloat16)


def local_block(inputs, b_proj, c_proj, step_size, log_decay):
    rows, heads, width = inputs.shape
    groups = b_proj.shape[1]
    per_group = heads // groups
    cumulative = jnp.cumsum(log_decay, axis=0)
    lower = jnp.arange(rows)[:, None] >= jnp.arange(rows)[None, :]
    grouped_x = jnp.moveaxis(inputs.reshape(rows, groups, per_group, width), 1, 0)
    grouped_cum = jnp.moveaxis(cumulative.reshape(rows, groups, per_group), 1, 0)
    grouped_dt = jnp.moveaxis(step_size.reshape(rows, groups, per_group), 1, 0)

    def per_head_group(items):
        x_grp, b_grp, c_grp, cum_grp, dt_grp = items
        scores = jnp.dot(c_grp, b_grp.T, preferred_element_type=jnp.float32)
        gap = cum_grp.T[:, :, None] - cum_grp.T[:, None, :]
        decay = jnp.where(lower, jnp.exp(jnp.where(lower, gap, 0.0)), 0.0)
        weights = (scores[None] * decay * dt_grp.T[:, None, :]).astype(jnp.bfloat16)
        intra = jnp.einsum("hts,shp->thp", weights, x_grp, preferred_element_type=jnp.float32)
        ending = jnp.exp(cum_grp[-1][None, :] - cum_grp) * dt_grp
        scaled = (x_grp.astype(jnp.float32) * ending[:, :, None]).astype(jnp.bfloat16)
        state = jnp.einsum("shp,sn->hpn", scaled, b_grp, preferred_element_type=jnp.float32)
        return (intra, state)

    intra, states = lax.map(
        per_head_group,
        (
            grouped_x,
            jnp.moveaxis(b_proj, 1, 0),
            jnp.moveaxis(c_proj, 1, 0),
            grouped_cum,
            grouped_dt,
        ),
    )
    intra = jnp.moveaxis(intra, 0, 1).reshape(rows, heads, width)
    return (intra, states.reshape(heads, width, -1), cumulative)


def state_part(c_proj, cumulative, state):
    rows, groups, _ = c_proj.shape
    heads = cumulative.shape[1]
    rounded = state.astype(jnp.bfloat16).reshape(groups, -1, state.shape[2])
    product = jnp.einsum("tgn,gkn->tgk", c_proj, rounded, preferred_element_type=jnp.float32)
    return product.reshape(rows, heads, -1) * jnp.exp(cumulative)[:, :, None]


def finish(mixer, inputs, gate_in, d_skip, norm_weight, live, groups):
    rows = mixer.shape[0]
    summed = mixer + d_skip[None, :, None] * inputs.astype(jnp.float32)
    gated = summed.reshape(rows, -1) * jax.nn.silu(gate_in.astype(jnp.float32))
    grouped = gated.reshape(rows, groups, -1)
    factor = lax.rsqrt(jnp.mean(grouped * grouped, axis=-1, keepdims=True) + 1e-05)
    normed = (grouped * factor).reshape(rows, -1) * norm_weight
    return jnp.where(live[:, None], normed, 0.0).astype(jnp.bfloat16)


def combine_pairs(earlier, later):
    return (earlier[0] * later[0], later[0][:, None, None] * earlier[1] + later[1])


def local(
    conv_input,
    gate_input,
    dt_raw,
    conv_weight,
    conv_bias,
    dt_bias,
    a_log,
    d_skip,
    norm_weight,
    conv_cache,
    state_pool,
    page_owner,
    page_slot,
    prefix_len,
    new_count,
):
    req_count = lax.axis_size("req")
    ctx_count = lax.axis_size("ctx")
    devices = req_count * ctx_count
    req_index = lax.axis_index("req")
    ctx_index = lax.axis_index("ctx")
    own_index = req_index * ctx_count + ctx_index
    tokens = conv_input[0]
    rows = tokens.shape[0]
    heads = dt_raw.shape[2]
    inner = gate_input.shape[2]
    width = inner // heads
    nstate = state_pool.shape[2]
    page_rows = state_pool.shape[1]
    pool_slots = state_pool.shape[0]
    head_share = heads // ctx_count
    device_pages = page_owner.shape[1] // ctx_count
    rim = conv_weight.shape[0] - 1
    prefix = prefix_len[req_index]
    count = new_count[req_index]
    owner_table = page_owner.reshape(devices, device_pages)
    slot_table = page_slot.reshape(devices, device_pages)
    matches = owner_table == own_index
    slot_for = jnp.sum(jnp.where(matches, slot_table, 0), axis=1)
    present = jnp.any(matches, axis=1)
    outgoing = jnp.where(present[:, None, None], state_pool[slot_for], 0.0)
    incoming = lax.all_to_all(outgoing, ("req", "ctx"), split_axis=0, concat_axis=0, tiled=True)
    my_owners = owner_table[own_index]
    initial_share = incoming[my_owners].reshape(head_share, width, nstate) * (prefix > 0).astype(
        jnp.float32
    )
    previous = passed_along(tokens[rows - rim :], "ctx", 1)
    keep_rows = jnp.arange(rim) >= rim - prefix
    cached = jnp.where(keep_rows[:, None], conv_cache[0], jnp.zeros_like(conv_cache[0]))
    rim_rows = jnp.where(ctx_index == 0, cached, previous)
    extended = jnp.concatenate([rim_rows, tokens], axis=0)
    active = conv_silu(extended, conv_weight, conv_bias, rows)
    groups = GROUPS
    inputs = active[:, :inner].reshape(rows, heads, width)
    b_proj = active[:, inner : inner + groups * nstate].reshape(rows, groups, nstate)
    c_proj = active[:, inner + groups * nstate :].reshape(rows, groups, nstate)
    positions = ctx_index * rows + jnp.arange(rows)
    live = positions < count
    step_size = jax.nn.softplus(dt_raw[0].astype(jnp.float32) + dt_bias) * live[:, None].astype(
        jnp.float32
    )
    log_decay = step_size * -jnp.exp(a_log)
    intra, states, cumulative = local_block(inputs, b_proj, c_proj, step_size, log_decay)
    decays = jnp.exp(cumulative[-1])
    all_decays = lax.all_gather(decays[None, :], "ctx", axis=0, tiled=True)
    block_ids = jnp.arange(ctx_count)
    initial = lax.all_gather(initial_share, "ctx", axis=0, tiled=True)
    before_decay, before_state = prefix_2(
        (decays, states), "ctx", combine_pairs, (jnp.ones_like(decays), jnp.zeros_like(states))
    )
    device_start = before_state + before_decay[:, None, None] * initial
    suffix = jnp.prod(jnp.where((block_ids > ctx_index)[:, None], all_decays, 1.0), axis=0)
    summed = lax.psum_scatter(
        (suffix[:, None, None] * states).astype(jnp.bfloat16),
        "ctx",
        scatter_dimension=0,
        tiled=True,
    ).astype(jnp.float32)
    whole_decay = lax.dynamic_slice_in_dim(
        jnp.prod(all_decays, axis=0), ctx_index * head_share, head_share, 0
    )
    final_share = summed + whole_decay[:, None, None] * initial_share
    carried = state_part(c_proj, cumulative, device_start)
    output = finish(intra + carried, inputs, gate_input[0], d_skip, norm_weight, live, groups)
    targets = count - rim + jnp.arange(rim)
    picks = (positions[None, :] == targets[:, None]).astype(jnp.bfloat16)
    tail_rows = jnp.dot(picks, tokens, preferred_element_type=jnp.float32)
    new_tail = lax.psum(tail_rows.astype(jnp.bfloat16), "ctx")
    final_pages = final_share.reshape(device_pages, page_rows, nstate)
    outbound = jnp.zeros((devices, page_rows, nstate), jnp.float32).at[my_owners].set(final_pages)
    returned = lax.all_to_all(
        outbound.astype(jnp.bfloat16), ("req", "ctx"), split_axis=0, concat_axis=0, tiled=True
    ).astype(outbound.dtype)
    target_slots = jnp.where(present, slot_for, pool_slots)
    new_pool = state_pool.at[target_slots].set(returned, mode="drop")
    return (output[None], new_tail[None], new_pool)


def solution(mesh):
    return jax.shard_map(
        local,
        mesh=mesh,
        in_specs=(
            P("req", "ctx", None),
            P("req", "ctx", None),
            P("req", "ctx", None),
            P(),
            P(),
            P(),
            P(),
            P(),
            P(),
            P("req", None, None),
            P(("req", "ctx"), None, None),
            P(),
            P(),
            P(),
            P(),
        ),
        out_specs=(P("req", "ctx", None), P("req", None, None), P(("req", "ctx"), None, None)),
        check_vma=False,
    )
```

profile of v0, /device:TPU:0, one launch (start us, length us, event | category | flops | bytes accessed | tf_op | source)
XLA Modules:
  0.0 331.9 jit_solution(16997944187443521749)
XLA Ops:
  7.2 4.7 %copy.85 = f32[32,256,128]{2,1,0:T(8,128)} copy(f32[32,256,128]{2,1,0:T(8,128)} %param.29) | data formatting | bytes 8388608
  15.3 8.0 %copy.44 = bf16[1,256,10240]{1,2,0:T(8,128)(2,1)} copy(bf16[1,256,10240]{2,1,0:T(8,128)(2,1)} %param.19) | data formatting | bytes 10485760 | tf_op args[0]
  36.1 15.6 %multiply_convert_fusion.7 = bf16[256,10240]{0,1:T(8,128)(2,1)S(1)} fusion(bf16[256,10240]{0,1:T(8,128)(2,1)S(1)} %bitcast.192, bf16[3,10240]{0,1:T(8,128)(2,1)S(1)} %fusion.45, f32[10240]{0:T(1024)S(1)} %bitcast.212, f32[10240]{0:T(1024)S(1)} %bitcast.213, f32[10240]{0:T(1024)S(1)} %bitcast.211, f32[10240]{0:T(1024)S(1)} %bitcast.210, f32[10240]{0:T(1024)S(1)} %copy-done.5), kind=kLoop, calls=%fused_computation.50 | loop fusion | flops 68157440 | bytes 10752000 | tf_op jit(solution)/shard_map/convert_element_type | solution.py:34
  55.7 50.0 %while.30 = (s32[]{:T(128)}, f32[8,256,16,64]{1,3,2,0:T(8,128)}, f32[8,16,64,128]{3,2,1,0:T(8,128)}, bf16[8,256,16,64]{1,3,2,0:T(8,128)(2,1)}, bf16[8,256,128]{1...) while((s32[]{:T(128)}, f32[8,256,16,64]{1,3,2,0:T(8,128)}, ...), condition=%wide.region_3.4_spmd.clone.clone, body=%wide.region_2.3_spmd.clone.clone.sunk | while | flops 225255424 | bytes 3657673 | solution.py:59
  68.4 3.6 %fusion.83 = f32[8,256,16,64]{1,3,2,0:T(8,128)} fusion(f32[8,256,16,64]{1,3,2,0:T(8,128)} %get-tuple-element.403, s32[]{:T(128)} %get-tuple-element.402, f32[16,256]{1,0:T(8,128)S(1)} %get-tuple-element.381, f32[16,256]{1,0:T(8,128)S(1)} %get-tuple-element.382, f32[256,256]{1,0:T(8,128)S(1)} %fusion.82, ...), kind=kOutput, calls=%fused_computation.14.clone.1 | convolution fusion | flops 140509184 | bytes 1950720 | tf_op jit(solution)/shard_map/while/body/eval_jaxpr/hts,shp->thp/dot_general | solution.py:53
  80.9 3.6 %fusion.83 = f32[8,256,16,64]{1,3,2,0:T(8,128)} fusion(f32[8,256,16,64]{1,3,2,0:T(8,128)} %get-tuple-element.403, s32[]{:T(128)} %get-tuple-element.402, f32[16,256]{1,0:T(8,128)S(1)} %get-tuple-element.381, f32[16,256]{1,0:T(8,128)S(1)} %get-tuple-element.382, f32[256,256]{1,0:T(8,128)S(1)} %fusion.82, ...), kind=kOutput, calls=%fused_computation.14.clone.1 | convolution fusion | flops 140509184 | bytes 1950720 | tf_op jit(solution)/shard_map/while/body/eval_jaxpr/hts,shp->thp/dot_general | solution.py:53
  93.4 3.6 %fusion.83 = f32[8,256,16,64]{1,3,2,0:T(8,128)} fusion(f32[8,256,16,64]{1,3,2,0:T(8,128)} %get-tuple-element.403, s32[]{:T(128)} %get-tuple-element.402, f32[16,256]{1,0:T(8,128)S(1)} %get-tuple-element.381, f32[16,256]{1,0:T(8,128)S(1)} %get-tuple-element.382, f32[256,256]{1,0:T(8,128)S(1)} %fusion.82, ...), kind=kOutput, calls=%fused_computation.14.clone.1 | convolution fusion | flops 140509184 | bytes 1950720 | tf_op jit(solution)/shard_map/while/body/eval_jaxpr/hts,shp->thp/dot_general | solution.py:53
  105.7 3.9 %fusion.44 = bf16[128,64,128]{2,1,0:T(8,128)(2,1)} fusion(f32[8,16,64,128]{3,2,1,0:T(8,128)} %get-tuple-element.165, f32[128]{0:T(128)S(1)} %select_reduce_fusion.1), kind=kLoop, calls=%fused_computation.72 | loop fusion | flops 2097152 | bytes 6291968 | tf_op jit(solution)/shard_map/convert_element_type | solution.py:169
  110.1 5.0 %gather_fusion = f32[32,256,128]{2,1,0:T(8,128)} fusion(f32[32,256,128]{2,1,0:T(8,128)} %copy.85, s32[1024]{0:T(1024)S(1)} %pad_clamp_fusion.1), kind=kCustom, calls=%fused_computation | custom fusion | bytes 8388736 | tf_op jit(solution)/shard_map/gather | solution.py:136
  115.1 4.8 %broadcast_select_fusion.2 = f32[32,256,128]{2,1,0:T(8,128)} fusion(f32[32,256,128]{2,1,0:T(8,128)} %gather_fusion, pred[32]{0:T(512)(128)(4,1)S(1)} %get-tuple-element.283), kind=kLoop, calls=%fused_computation.77 | loop fusion | flops 1048576 | bytes 8388640 | tf_op jit(solution)/shard_map/jit(_where)/select_n | solution.py:136
  119.9 7.9 %all-to-all-start = ((f32[32,256,128]{2,1,0:T(8,128)}), f32[32,256,128]{2,1,0:T(8,128)}, u32[]{:S(2)}, u32[]{:S(2)}) async-start(f32[32,256,128]{2,1,0:T(8,128)} %broadcast_select_fusion.2), calls=%async_computation | async-start | bytes 8388608 | tf_op jit(solution)/shard_map/all_to_all | solution.py:137
  129.3 92.3 %all-to-all-done = f32[32,256,128]{2,1,0:T(8,128)} async-done(((f32[32,256,128]{2,1,0:T(8,128)}), f32[32,256,128]{2,1,0:T(8,128)}, u32[]{:S(2)}, u32[]{:S(2)}) %all-to-all-start) | async-done | bytes 4194336 | tf_op jit(solution)/shard_map/all_to_all | solution.py:137
  230.7 4.0 %scatter_fusion = f32[32,256,128]{2,1,0:T(8,128)} fusion(f32[32,256,128]{2,1,0:T(8,128)} %broadcast_in_dim.133, s32[16]{0:T(128)S(1)} %fusion.55, f32[16,256,128]{2,1,0:T(8,128)S(1)} %bitcast.198), kind=kCustom, calls=%fused_computation.2 | custom fusion | bytes 6291520 | tf_op jit(solution)/shard_map/scatter | solution.py:185
  234.6 4.6 %convert_element_type.106 = bf16[32,256,128]{2,1,0:T(8,128)(2,1)} convert(f32[32,256,128]{2,1,0:T(8,128)} %scatter_fusion) | non-fusion elementwise | flops 1048576 | bytes 6291456 | tf_op jit(solution)/shard_map/convert_element_type | solution.py:187
  242.9 6.4 %copy.54 = bf16[1,256,8192]{1,2,0:T(8,128)(2,1)} copy(bf16[1,256,8192]{2,1,0:T(8,128)(2,1)} %param.20) | data formatting | bytes 8388608 | tf_op args[1]
  253.5 4.4 %psum.7 = bf16[1,3,10240]{2,1,0:T(4,128)(2,1)} all-reduce(bf16[1,3,10240]{2,1,0:T(4,128)(2,1)S(1)} %fusion.31), channel_id=1, replica_groups=mesh['req'=16,'ctx'=2] {'ctx'}, use_global_device_ids=true, to_apply=%region_9.10 | all-reduce | flops 30720 | bytes 122880 | tf_op jit(solution)/shard_map/psum | solution.py:183
  257.9 10.8 %while.31 = (s32[]{:T(128)}, f32[128]{0:T(128)S(1)}, f32[128,64,128]{2,1,0:T(8,128)}, s32[]{:T(128)}, f32[2,128]{1,0:T(2,128)S(1)}, /*index=5*/f32[2,128,64,128]{3,2,1,0:T(8,128)}, s32[]{:T(128)}, s32[]{:T(128)}) while((s32[]{:T(128)}, f32[128]{0:T(128)S(1)}, f32[128,64,128]{2,1,0:T(8,128)}, s32[]{:T(128)}, ...), condition=%wide.region_5.6_spmd.clone, body=%wide.region_4.5_spmd.clone.sunk | while | flops 4194692 | bytes 12585587 | solution.py:27
  257.9 4.7 %fusion.85 = f32[128,64,128]{2,1,0:T(8,128)} fusion(f32[2,128,64,128]{3,2,1,0:T(8,128)} %get-tuple-element.445, s32[]{:T(128)} %get-tuple-element.432, f32[128,64,128]{2,1,0:T(8,128)} %get-tuple-element.434, f32[128]{0:T(128)S(1)} %get-tuple-element.390, pred[]{:T(512)S(6)} %compare.3, pred[]{:T(512)S(6)} %lt.103), kind=kLoop, calls=%fused_computation.42.clone.1 | loop fusion | flops 4194304 | bytes 12583430 | tf_op jit(solution)/shard_map/while/body/eval_jaxpr/jit(_where)/select_n | solution.py:25
  262.7 6.0 %fusion.85 = f32[128,64,128]{2,1,0:T(8,128)} fusion(f32[2,128,64,128]{3,2,1,0:T(8,128)} %get-tuple-element.445, s32[]{:T(128)} %get-tuple-element.432, f32[128,64,128]{2,1,0:T(8,128)} %get-tuple-element.434, f32[128]{0:T(128)S(1)} %get-tuple-element.390, pred[]{:T(512)S(6)} %compare.3, pred[]{:T(512)S(6)} %lt.103), kind=kLoop, calls=%fused_computation.42.clone.1 | loop fusion | flops 4194304 | bytes 12583430 | tf_op jit(solution)/shard_map/while/body/eval_jaxpr/jit(_where)/select_n | solution.py:25
  268.7 23.0 %all-to-all-done.1 = bf16[32,256,128]{2,1,0:T(8,128)(2,1)S(1)} async-done(((bf16[32,256,128]{2,1,0:T(8,128)(2,1)}), bf16[32,256,128]{2,1,0:T(8,128)(2,1)S(1)}, u32[]{:S(2)}, u32[]{:S(2)}) %all-to-all-start.1) | async-done | bytes 2097184 | tf_op jit(solution)/shard_map/all_to_all | solution.py:186
  294.3 7.9 %scatter_fusion.1 = f32[32,256,128]{2,1,0:T(8,128)} fusion(f32[32,256,128]{2,1,0:T(8,128)} %copy.85, s32[32]{0:T(128)S(1)} %get-tuple-element.295, f32[32,256,128]{2,1,0:T(8,128)} %convert_element_type.107), kind=kCustom, calls=%fused_computation.3 | custom fusion | bytes 12583040 | tf_op jit(solution)/shard_map/scatter | solution.py:190
  302.2 4.1 %add_convert_fusion = bf16[128,64,128]{2,1,0:T(8,128)(2,1)S(1)} fusion(f32[128,64,128]{2,1,0:T(8,128)} %get-tuple-element.166, f32[128,64,128]{2,1,0:T(8,128)} %all-gather.6.cloned.1.call-done, f32[128]{0:T(128)S(1)} %get-tuple-element.167), kind=kLoop, calls=%fused_computation.73 | loop fusion | flops 3145728 | bytes 10486272 | tf_op jit(solution)/shard_map/convert_element_type | solution.py:76
  309.7 6.7 %bitcast_reduce_fusion = (f32[256,8]{0,1:T(8,128)S(1)}, f32[256,8192]{0,1:T(8,128)S(1)}) fusion(bf16[1,256,8192]{1,2,0:T(8,128)(2,1)S(1)} %copy-done.1, bf16[256,10240]{0,1:T(8,128)(2,1)S(1)} %bitcast.189, f32[8192]{0:T(1024)S(1)} %mul.254, f32[256,128]{0,1:T(8,128)S(1)} %copy.53, f32[8,1024,256]{2,1,0:T(8,128)S(1)} %fusion.64, ...), kind=kLoop, calls=%fused_computation.64 | loop fusion | flops 27260928 | bytes 33726464 | tf_op jit(solution)/shard_map/reduce_sum | solution.py:86
  319.0 6.3 %copy.55 = bf16[1,256,8192]{2,1,0:T(8,128)(2,1)} copy(bf16[1,256,8192]{1,2,0:T(8,128)(2,1)} %bitcast.196) | data formatting | bytes 8388608
  (173 shorter events, 84.4 us)
Async XLA Ops:
  7.2 218.9 %reduce-scatter.2.cloned.1.call-start = ((), (), s32[]{:S(2)}) async-start(), calls=%async_computation.5 | async-start | bytes 3145728 | tf_op jit(solution)/shard_map/reduce_scatter | solution.py:168
  12.8 18.2 %collective-permute-start = (bf16[3,10240]{1,0:T(4,128)(2,1)S(1)}, bf16[3,10240]{1,0:T(4,128)(2,1)S(1)}, u32[]{:S(2)}, u32[]{:S(2)}) collective-permute-start(bf16[3,10240]{1,0:T(4,128)(2,1)S(1)} %slice_bitcast_fusion), channel_id=1, source_target_pairs={{0,1},{2,3},{4,5},{6,7},{8,9},{10,11},{12,13},{14,15},{16,17},{18,... | collective-permute-start | bytes 184328 | tf_op jit(solution)/shard_map/ppermute | solution.py:12
  15.2 8.1 %copy-start.4 = (bf16[1,256,128]{2,1,0:T(8,128)(2,1)S(1)}, bf16[1,256,128]{2,1,0:T(8,128)(2,1)}, u32[]{:S(2)}) copy-start(bf16[1,256,128]{2,1,0:T(8,128)(2,1)} %param.21) | copy-start | bytes 196612
  15.2 8.2 %copy-start.11 = (f32[128]{0:T(128)S(1)}, f32[128]{0:T(128)}, u32[]{:S(2)}) copy-start(f32[128]{0:T(128)} %param.25) | copy-start | bytes 1540
  15.2 8.2 %copy-start.9 = (f32[128]{0:T(128)S(1)}, f32[128]{0:T(128)}, u32[]{:S(2)}) copy-start(f32[128]{0:T(128)} %param.24) | copy-start | bytes 1540
  15.2 8.3 %copy-start.12 = (s32[16]{0:T(128)S(1)}, s32[16]{0:T(128)}, u32[]{:S(2)}) copy-start(s32[16]{0:T(128)} %param.33) | copy-start | bytes 196
  15.2 10.3 %copy-start.13 = (s32[16]{0:T(128)S(1)}, s32[16]{0:T(128)}, u32[]{:S(2)}) copy-start(s32[16]{0:T(128)} %param.32) | copy-start | bytes 196
  15.3 10.9 %copy-start.3 = (bf16[1,3,10240]{2,1,0:T(4,128)(2,1)S(1)}, bf16[1,3,10240]{2,1,0:T(4,128)(2,1)}, u32[]{:S(2)}) copy-start(bf16[1,3,10240]{2,1,0:T(4,128)(2,1)} %param.28) | copy-start | bytes 184324
  23.3 5.0 %copy-start.2 = (f32[4,10240]{1,0:T(4,128)S(1)}, f32[4,10240]{1,0:T(4,128)}, u32[]{:S(2)}) copy-start(f32[4,10240]{1,0:T(4,128)} %param.22) | copy-start | bytes 491524
  31.0 4.1 %slice-start.2 = ((s8[5242880]{0:T(1024)(128)(4,1)}), s8[1048576]{0:T(1024)(128)(4,1)S(1)}, s32[]{:S(2)}) async-start(s8[5242880]{0:T(1024)(128)(4,1)} %bitcast.190), calls=%async_computation.8 | async-start | bytes 2097152
  33.1 3.0 slice-start.3
  33.2 3.0 copy-start.5
  51.8 3.7 %copy-start = (bf16[256,10240]{0,1:T(8,128)(2,1)}, bf16[256,10240]{0,1:T(8,128)(2,1)S(1)}, u32[]{:S(2)}) copy-start(bf16[256,10240]{0,1:T(8,128)(2,1)S(1)} %multiply_convert_fusion.7) | copy-start | bytes 15728644
  105.7 4.0 %copy-start.7 = (s32[16,32]{1,0:T(8,128)S(1)}, s32[16,32]{1,0:T(8,128)}, u32[]{:S(2)}) copy-start(s32[16,32]{1,0:T(8,128)} %param.30) | copy-start | bytes 6148
  105.7 4.0 %copy-start.8 = (s32[16,32]{1,0:T(8,128)S(1)}, s32[16,32]{1,0:T(8,128)}, u32[]{:S(2)}) copy-start(s32[16,32]{1,0:T(8,128)} %param.31) | copy-start | bytes 6148
  119.9 101.8 %all-to-all-start = ((f32[32,256,128]{2,1,0:T(8,128)}), f32[32,256,128]{2,1,0:T(8,128)}, u32[]{:S(2)}, u32[]{:S(2)}) async-start(f32[32,256,128]{2,1,0:T(8,128)} %broadcast_select_fusion.2), calls=%async_computation | async-start | bytes 8388608 | tf_op jit(solution)/shard_map/all_to_all | solution.py:137
  127.7 130.2 %all-gather.4.cloned.1.call-start = ((), (), s32[]{:S(2)}) async-start(), calls=%async_computation.3 | async-start | bytes 12582912 | tf_op jit(solution)/shard_map/all_gather | solution.py:17
  128.5 173.7 %all-gather.6.cloned.1.call-start = ((), (), s32[]{:S(2)}) async-start(), calls=%async_computation.4 | async-start | bytes 6291456 | tf_op jit(solution)/shard_map/all_gather | solution.py:162
  239.2 52.4 %all-to-all-start.1 = ((bf16[32,256,128]{2,1,0:T(8,128)(2,1)}), bf16[32,256,128]{2,1,0:T(8,128)(2,1)S(1)}, u32[]{:S(2)}, u32[]{:S(2)}) async-start(bf16[32,256,128]{2,1,0:T(8,128)(2,1)} %convert_element_type.106), calls=%async_computation.2 | async-start | bytes 4194304 | tf_op jit(solution)/shard_map/all_to_all | solution.py:186
  242.9 6.4 %copy-start.10 = (f32[128]{0:T(128)S(1)}, f32[128]{0:T(128)}, u32[]{:S(2)}) copy-start(f32[128]{0:T(128)} %param.26) | copy-start | bytes 1540
  302.2 5.3 %slice-start = ((s8[5242880]{0:T(1024)(128)(4,1)}), s8[1048576]{0:T(1024)(128)(4,1)S(1)}, s32[]{:S(2)}) async-start(s8[5242880]{0:T(1024)(128)(4,1)} %bitcast.188), calls=%async_computation.6 | async-start | bytes 2097152
  306.3 2.2 slice-start.1
  306.3 3.5 %copy-start.1 = (bf16[1,256,8192]{1,2,0:T(8,128)(2,1)S(1)}, bf16[1,256,8192]{1,2,0:T(8,128)(2,1)}, u32[]{:S(2)}) copy-start(bf16[1,256,8192]{1,2,0:T(8,128)(2,1)} %copy.54) | copy-start | bytes 12582916
  309.7 6.7 %copy-start.6 = (f32[8192]{0:T(1024)S(1)}, f32[8192]{0:T(1024)}, u32[]{:S(2)}) copy-start(f32[8192]{0:T(1024)} %param.27) | copy-start | bytes 98308
Sparse Core Ops, SparseCore 0:
  109.8 12.3 reduce-scatter.1
  130.2 21.0 all-gather.3
  226.1 13.0 all-gather.5
where the time goes:
time: 334 us; the launch traced here: 332 us
  waiting for transfers between devices  116 us (35%)
  other arithmetic  63.7 us (19%)
  local copies, waits for them, and re-layouts  63.4 us (19%)
  matrix products  52.2 us (16%)
  between operations  16.2 us (5%)
  starting transfers between devices  13.9 us (4%)
  blocking collectives  6.18 us (2%)
    all_to_all x1, waiting for transfers between devices, local(): lax.all_to_all(outgoing, ('req', 'ctx'), split_axis=0, concat_axis=0, til...  92.3 us
    unnamed x44, local copies, waits for them, and re-layouts  31.8 us
    dot_general x8, matrix products, per_head_group(): jnp.einsum('hts,shp->thp', weights, x_grp, preferred_element_type=jnp.flo...  28.8 us
    all_to_all x1, waiting for transfers between devices, local(): lax.all_to_all(outbound.astype(jnp.bfloat16), ('req', 'ctx'), split_axis=...  23 us
    dot_general x8, matrix products, per_head_group(): jnp.einsum('shp,sn->hpn', scaled, b_grp, preferred_element_type=jnp.float32)  17.3 us
    convert_element_type x1, other arithmetic, conv_silu(): return jax.nn.silu(accum).astype(jnp.bfloat16)  15.6 us
    select_n x4, other arithmetic, step(): return jax.tree.map(lambda a, b: jnp.where(reached, a, b), new, before)  10.7 us
    scatter x1, local copies, waits for them, and re-layouts, local(): new_pool = state_pool.at[target_slots].set(returned, mode='drop')  7.91 us
  transfers between devices with their start and end apart: 6, of which 2 were waited for; matrix products, arithmetic and copies ran while one was open for 22% of the time, Pallas kernels for 0%

commit v1 on v0

v1 whole, which is shorter than its diff:
```python
import functools

import jax
import jax.numpy as jnp
from jax import lax
from jax.experimental import pallas as pl
from jax.experimental.pallas import tpu as pltpu
from jax.sharding import PartitionSpec as P

GROUPS = 8
F32 = jnp.float32
BF16 = jnp.bfloat16
NT = (((1,), (1,)), ((), ()))
TN = (((0,), (0,)), ((), ()))


def params(mib):
    return pltpu.CompilerParams(vmem_limit_bytes=mib * 1024 * 1024)


def cost(flops, moved):
    return pl.CostEstimate(flops=flops, bytes_accessed=moved, transcendentals=0)


def fetch_kernel(slots, pool, out):
    first = pl.program_id(0) * out.shape[0]

    def one(i, carry):
        out[i] = pool[slots[first + i]].astype(BF16)
        return carry

    lax.fori_loop(0, out.shape[0], one, 0)


def fetch_pages(pool, slots):
    count = slots.shape[0]
    steps = 4
    return pl.pallas_call(
        fetch_kernel,
        grid_spec=pltpu.PrefetchScalarGridSpec(
            num_scalar_prefetch=1,
            grid=(steps,),
            in_specs=[pl.BlockSpec(pool.shape, lambda i, s: (0, 0, 0))],
            out_specs=pl.BlockSpec((count // steps,) + pool.shape[1:], lambda i, s: (i, 0, 0)),
        ),
        out_shape=jax.ShapeDtypeStruct((count,) + pool.shape[1:], BF16),
        compiler_params=params(32),
        cost_estimate=cost(0, 6 * 2**20),
        name="fetch_pages",
    )(slots, pool)


def block_kernel(
    xin, bin_, cin, rimx, rimb, rimc, wx, wb, wc, ax, ab, ac, cl, clt, dtt, end, skip,
    y_ref, st_ref, c_ref, ext,
):
    rows, wide = xin.shape[1:]
    nstate = bin_.shape[2]
    taps = wx.shape[0]
    pad = rimx.shape[0]
    half = rows // 2
    for at, body, rim in ((0, xin, rimx), (wide, bin_, rimb), (wide + nstate, cin, rimc)):
        size = body.shape[2]
        ext[0:pad, at : at + size] = rim[...]
        ext[pad : pad + rows, at : at + size] = body[0].astype(F32)

    def act(at, col, size, weight, bias):
        accum = jnp.broadcast_to(bias[:, col : col + size], (rows, size))
        for k in range(taps):
            start = pad - taps + 1 + k
            piece = ext[start : start + rows, at + col : at + col + size]
            accum = accum + weight[k : k + 1, col : col + size] * piece
        return jax.nn.silu(accum).astype(BF16)

    b = act(wide, 0, nstate, wb, ab)
    c = act(wide + nstate, 0, nstate, wc, ac)
    c_ref[...] = c
    scores = lax.dot_general(c, b, NT, preferred_element_type=F32)
    row_id = lax.broadcasted_iota(jnp.int32, (half, half), 0)
    col_id = lax.broadcasted_iota(jnp.int32, (half, half), 1)
    lower = row_id >= col_id
    left = lax.broadcasted_iota(jnp.int32, (half, 128), 1) < 64
    left_all = lax.broadcasted_iota(jnp.int32, (rows, 128), 1) < 64
    for pair in range(wide // 128):
        cols = slice(pair * 128, pair * 128 + 128)
        x = act(0, pair * 128, 128, wx, ax)
        xf = x.astype(F32)
        tops, bottoms = [], []
        for head in (2 * pair, 2 * pair + 1):
            down = cl[0, :, head : head + 1]
            across = clt[head : head + 1, :]
            dt = dtt[head : head + 1, :]

            def part(r, s, diagonal):
                gap = down[r * half : (r + 1) * half] - across[:, s * half : (s + 1) * half]
                if diagonal:
                    gap = jnp.where(lower, gap, -1e30)
                value = scores[r * half : (r + 1) * half, s * half : (s + 1) * half] * jnp.exp(gap)
                return (value * dt[:, s * half : (s + 1) * half]).astype(BF16)

            tops.append(jnp.dot(part(0, 0, True), x[:half], preferred_element_type=F32))
            low = jnp.concatenate([part(1, 0, False), part(1, 1, True)], axis=1)
            bottoms.append(jnp.dot(low, x, preferred_element_type=F32))
        y_ref[0:half, cols] = jnp.where(left, tops[0], tops[1]) + skip[:, cols] * xf[:half]
        y_ref[half:rows, cols] = jnp.where(left, bottoms[0], bottoms[1]) + skip[:, cols] * xf[half:]
        ending = jnp.where(
            left_all, end[0, :, 2 * pair : 2 * pair + 1], end[0, :, 2 * pair + 1 : 2 * pair + 2]
        )
        scaled = (xf * ending).astype(BF16)
        st_ref[pair * 128 : pair * 128 + 128, :] = lax.dot_general(
            scaled, b, TN, preferred_element_type=F32
        ).astype(BF16)


def block_work(conv_input, rim8, conv_weight, conv_bias, cl_g, clt, dtt, end_g, skip, inner, nstate):
    rows, dim = conv_input.shape[1:]
    taps = conv_weight.shape[0]
    wide = inner // GROUPS
    per = cl_g.shape[2]
    first_b = inner // nstate
    first_c = first_b + GROUPS
    bias = conv_bias[None, :]

    def three(lead, block_rows):
        zero = (0,) * len(lead)
        return [
            pl.BlockSpec(lead + (block_rows, wide), lambda g: zero + (0, g)),
            pl.BlockSpec(lead + (block_rows, nstate), lambda g: zero + (0, first_b + g)),
            pl.BlockSpec(lead + (block_rows, nstate), lambda g: zero + (0, first_c + g)),
        ]

    by_group = pl.BlockSpec((1, rows, per), lambda g: (g, 0, 0))
    by_rows = pl.BlockSpec((per, rows), lambda g: (g, 0))
    return pl.pallas_call(
        block_kernel,
        grid=(GROUPS,),
        in_specs=three((1,), rows)
        + three((), 8)
        + three((), taps)
        + three((), 1)
        + [by_group, by_rows, by_rows, by_group, pl.BlockSpec((1, wide), lambda g: (0, g))],
        out_specs=[
            pl.BlockSpec((rows, wide), lambda g: (0, g)),
            pl.BlockSpec((wide, nstate), lambda g: (g, 0)),
            pl.BlockSpec((rows, nstate), lambda g: (0, g)),
        ],
        out_shape=[
            jax.ShapeDtypeStruct((rows, inner), F32),
            jax.ShapeDtypeStruct((inner, nstate), BF16),
            jax.ShapeDtypeStruct((rows, GROUPS * nstate), BF16),
        ],
        scratch_shapes=[pltpu.VMEM((rows + 8, wide + 2 * nstate), F32)],
        compiler_params=params(32),
        cost_estimate=cost(30 * 10**9, 40 * 2**20),
        name="block_work",
    )(
        *([conv_input] * 3), *([rim8] * 3), *([conv_weight] * 3), *([bias] * 3),
        cl_g, clt, dtt, end_g, skip,
    )


def finish_kernel(count, y, c, rst, cl, gate, gain, out, g_ref):
    rows, wide = y.shape
    grown = jnp.exp(cl[0])
    left = lax.broadcasted_iota(jnp.int32, (rows, 128), 1) < 64
    squares = jnp.zeros((rows, 128), F32)
    for pair in range(wide // 128):
        cols = slice(pair * 128, pair * 128 + 128)
        carried = lax.dot_general(c[...], rst[cols, :], NT, preferred_element_type=F32)
        growth = jnp.where(left, grown[:, 2 * pair : 2 * pair + 1], grown[:, 2 * pair + 1 : 2 * pair + 2])
        g = (y[:, cols] + carried * growth) * jax.nn.silu(gate[0, :, cols].astype(F32))
        g_ref[:, cols] = g
        squares = squares + g * g
    mean = jnp.sum(squares, axis=1, keepdims=True) / wide
    live = lax.broadcasted_iota(jnp.int32, (rows, 1), 0) < count[0]
    factor = jnp.where(live, lax.rsqrt(mean + 1e-05), 0.0)
    for pair in range(wide // 128):
        cols = slice(pair * 128, pair * 128 + 128)
        out[0, :, cols] = (g_ref[:, cols] * factor * gain[:, cols]).astype(BF16)


def finish(count, y, c, rst, cl_g, gate, gain):
    rows, inner = y.shape
    wide = inner // GROUPS
    nstate = rst.shape[1]
    per = cl_g.shape[2]
    return pl.pallas_call(
        finish_kernel,
        grid_spec=pltpu.PrefetchScalarGridSpec(
            num_scalar_prefetch=1,
            grid=(GROUPS,),
            in_specs=[
                pl.BlockSpec((rows, wide), lambda g, s: (0, g)),
                pl.BlockSpec((rows, nstate), lambda g, s: (0, g)),
                pl.BlockSpec((wide, nstate), lambda g, s: (g, 0)),
                pl.BlockSpec((1, rows, per), lambda g, s: (g, 0, 0)),
                pl.BlockSpec((1, rows, wide), lambda g, s: (0, 0, g)),
                pl.BlockSpec((1, wide), lambda g, s: (0, g)),
            ],
            out_specs=pl.BlockSpec((1, rows, wide), lambda g, s: (0, 0, g)),
            scratch_shapes=[pltpu.VMEM((rows, wide), F32)],
        ),
        out_shape=jax.ShapeDtypeStruct((1, rows, inner), BF16),
        compiler_params=params(32),
        cost_estimate=cost(10 * 10**9, 40 * 2**20),
        name="finish",
    )(count, y, c, rst, cl_g, gate, gain)


def combine_kernel(pages, scale_a, scale_b, a, b, out):
    _, page_rows, _ = out.shape
    width = a.shape[0] // scale_a.shape[0]
    per = page_rows // width

    def one(i, carry):
        page = pages[pl.program_id(0) * out.shape[0] + i]
        for h in range(per):
            head = page * per + h
            rows = pl.ds(pl.multiple_of(head * width, width), width)
            total = a[rows, :].astype(F32) * scale_a[head] + b[rows, :].astype(F32) * scale_b[head]
            out[i, h * width : (h + 1) * width, :] = total.astype(BF16)
        return carry

    lax.fori_loop(0, out.shape[0], one, 0)


def combine(pages, scale_a, scale_b, a, b, page_rows):
    devices = pages.shape[0]
    nstate = a.shape[1]
    steps = 2
    whole = pl.BlockSpec(a.shape, lambda i, *s: (0, 0))
    return pl.pallas_call(
        combine_kernel,
        grid_spec=pltpu.PrefetchScalarGridSpec(
            num_scalar_prefetch=3,
            grid=(steps,),
            in_specs=[whole, whole],
            out_specs=pl.BlockSpec((devices // steps, page_rows, nstate), lambda i, *s: (i, 0, 0)),
        ),
        out_shape=jax.ShapeDtypeStruct((devices, page_rows, nstate), BF16),
        compiler_params=params(32),
        cost_estimate=cost(0, 6 * 2**20),
        name="combine",
    )(pages, scale_a, scale_b, a, b)


def store_kernel(source, used, decay, pool, back, out):
    slots, page_rows, _ = out.shape
    per = decay.shape[1]
    width = page_rows // per

    def one(i, carry):
        slot = pl.program_id(0) * slots + i
        for h in range(per):
            rows = slice(h * width, (h + 1) * width)
            part = back[source[slot], rows, :].astype(F32)
            part = jnp.where(used[slot] > 0, part, 0.0)
            out[i, rows, :] = pool[i, rows, :] * decay[slot, h] + part
        return carry

    lax.fori_loop(0, slots, one, 0)


def store_pages(source, used, decay, pool, back):
    slots, page_rows, nstate = pool.shape
    steps = 4
    block = pl.BlockSpec((slots // steps, page_rows, nstate), lambda i, *s: (i, 0, 0))
    return pl.pallas_call(
        store_kernel,
        grid_spec=pltpu.PrefetchScalarGridSpec(
            num_scalar_prefetch=3,
            grid=(steps,),
            in_specs=[block, pl.BlockSpec(back.shape, lambda i, *s: (0, 0, 0))],
            out_specs=block,
        ),
        out_shape=jax.ShapeDtypeStruct(pool.shape, F32),
        compiler_params=params(32),
        cost_estimate=cost(0, 10 * 2**20),
        name="store_pages",
    )(source, used, decay, pool, back)


def local(
    conv_input,
    gate_input,
    dt_raw,
    conv_weight,
    conv_bias,
    dt_bias,
    a_log,
    d_skip,
    norm_weight,
    conv_cache,
    state_pool,
    page_owner,
    page_slot,
    prefix_len,
    new_count,
):
    req_count = lax.axis_size("req")
    ctx_count = lax.axis_size("ctx")
    devices = req_count * ctx_count
    req_index = lax.axis_index("req")
    ctx_index = lax.axis_index("ctx")
    own_index = req_index * ctx_count + ctx_index
    swap = [(0, 1), (1, 0)]
    tokens = conv_input[0]
    rows = tokens.shape[0]
    heads = dt_raw.shape[2]
    inner = gate_input.shape[2]
    width = inner // heads
    pool_slots, page_rows, nstate = state_pool.shape
    device_pages = page_owner.shape[1] // ctx_count
    page_heads = page_rows // width
    rim = conv_weight.shape[0] - 1
    per_group = heads // GROUPS
    prefix = prefix_len[req_index]
    count = new_count[req_index]
    owner_table = page_owner.reshape(devices, device_pages)
    slot_table = page_slot.reshape(devices, device_pages)
    page_ids = jnp.arange(device_pages, dtype=jnp.int32)
    matches = owner_table == own_index
    slot_for = jnp.sum(jnp.where(matches, slot_table, 0), axis=1)
    page_for = jnp.sum(jnp.where(matches, page_ids[None, :], 0), axis=1)
    present = jnp.any(matches, axis=1)
    incoming = lax.all_to_all(
        fetch_pages(state_pool, slot_for), ("req", "ctx"), split_axis=0, concat_axis=0, tiled=True
    )
    my_owners = owner_table[own_index]

    previous = lax.ppermute(tokens[rows - rim :], "ctx", [(0, 1)])
    keep_rows = jnp.arange(rim) >= rim - prefix
    cached = jnp.where(keep_rows[:, None], conv_cache[0], jnp.zeros_like(conv_cache[0]))
    rim_rows = jnp.where(ctx_index == 0, cached, previous)
    rim8 = jnp.concatenate([jnp.zeros((8 - rim, tokens.shape[1]), F32), rim_rows.astype(F32)], axis=0)

    positions = ctx_index * rows + jnp.arange(rows)
    live = positions < count
    step_size = jax.nn.softplus(dt_raw[0].astype(F32) + dt_bias) * live[:, None].astype(F32)
    cumulative = jnp.cumsum(step_size * -jnp.exp(a_log), axis=0)
    ending = jnp.exp(cumulative[-1][None, :] - cumulative) * step_size
    all_ends = jnp.exp(lax.all_gather(cumulative[-1], ("req", "ctx"), axis=0))
    by_request = all_ends.reshape(req_count, ctx_count, heads)

    def grouped(array):
        return jnp.moveaxis(array.reshape(rows, GROUPS, per_group), 1, 0)

    cl_g = grouped(cumulative)
    y, states, c_proj = block_work(
        conv_input, rim8, conv_weight, conv_bias, cl_g, cumulative.T, step_size.T,
        grouped(ending), jnp.repeat(d_skip, width)[None, :], inner, nstate,
    )

    share = inner // ctx_count
    head_share = heads // ctx_count
    mine = lax.dynamic_slice_in_dim(states, ctx_index * share, share, 0)
    theirs = lax.dynamic_slice_in_dim(states, (1 - ctx_index) * share, share, 0)
    other = lax.ppermute(theirs, "ctx", swap)
    later = lax.dynamic_slice_in_dim(by_request[req_index, 1], ctx_index * head_share, head_share, 0)
    ones = jnp.ones_like(later)
    outbound = combine(
        jnp.sum(
            jnp.where(my_owners[None, :] == jnp.arange(devices)[:, None], page_ids[None, :], 0), axis=1
        ),
        jnp.where(ctx_index == 0, later, ones),
        jnp.where(ctx_index == 0, ones, later),
        mine,
        other,
        page_rows,
    )
    returned = lax.all_to_all(outbound, ("req", "ctx"), split_axis=0, concat_axis=0, tiled=True)

    first_half = lax.ppermute(states[:share], "ctx", [(0, 1)])
    before = jnp.concatenate([first_half, jnp.where(ctx_index == 0, jnp.zeros_like(other), other)], axis=0)
    initial = lax.all_gather(incoming[my_owners].reshape(share, nstate), "ctx", axis=0, tiled=True)
    factor = jnp.where(ctx_index == 0, 1.0, by_request[req_index, 0]) * (prefix > 0).astype(F32)
    start = (
        initial.astype(F32).reshape(heads, width, nstate) * factor[:, None, None]
        + before.astype(F32).reshape(heads, width, nstate)
    ).astype(BF16)
    mixed = finish(
        (count - ctx_index * rows).reshape(1),
        y, c_proj, start.reshape(inner, nstate), cl_g, gate_input, norm_weight[None, :],
    )

    targets = count - rim + jnp.arange(rim) - ctx_index * rows
    inside = (targets >= 0) & (targets < rows)
    tail = jnp.where(inside[:, None], tokens[jnp.clip(targets, 0, rows - 1)], jnp.zeros((), BF16))
    new_tail = tail + lax.ppermute(tail, "ctx", swap)

    total = jnp.prod(by_request, axis=1) * (prefix_len > 0).astype(F32)[:, None]
    paged = total.reshape(devices, device_pages, page_heads)
    chosen = (page_for[:, None] == page_ids[None, :])[:, :, None]
    page_decay = jnp.sum(jnp.where(chosen, paged, 0.0), axis=1)
    hit = (slot_for[None, :] == jnp.arange(pool_slots)[:, None]) & present[None, :]
    used = jnp.any(hit, axis=1)
    source = jnp.sum(jnp.where(hit, jnp.arange(devices, dtype=jnp.int32)[None, :], 0), axis=1)
    slot_decay = jnp.sum(jnp.where(hit[:, :, None], page_decay[None], 0.0), axis=1)
    slot_decay = jnp.where(used[:, None], slot_decay, 1.0)
    new_pool = store_pages(source, used.astype(jnp.int32), slot_decay, state_pool, returned)
    return (mixed, new_tail[None], new_pool)


def solution(mesh):
    return jax.shard_map(
        local,
        mesh=mesh,
        in_specs=(
            P("req", "ctx", None),
            P("req", "ctx", None),
            P("req", "ctx", None),
            P(),
            P(),
            P(),
            P(),
            P(),
            P(),
            P("req", None, None),
            P(("req", "ctx"), None, None),
            P(),
            P(),
            P(),
            P(),
        ),
        out_specs=(P("req", "ctx", None), P("req", None, None), P(("req", "ctx"), None, None)),
        check_vma=False,
    )
```

time: 334 us -> 196 us (0.59)
  waiting for transfers between devices: 116 us -> 34.6 us
  matrix products: 52.2 us -> 0 us
  other arithmetic: 63.7 us -> 15.4 us
  Pallas kernels: 0 us -> 40.9 us
  blocking collectives: 6.18 us -> 41.5 us
  local copies, waits for them, and re-layouts: 63.4 us -> 29.6 us
    all_to_all x2, waiting for transfers between devices: 115 us -> 34.5 us  [the longest x1 34.5 us: local(): lax.all_to_all(outbound, ('req', 'ctx'), split_axis=0, concat_axis=0, til...]
    dot_general x26 -> x0, matrix products: 52.2 us -> none  [the longest x8 28.8 us: per_head_group(): jnp.einsum('hts,shp->thp', weights, x_grp, preferred_element_type=jnp.flo...]
    pallas_call x0 -> x5, Pallas kernels: none -> 40.9 us  [the longest x1 23.1 us: block_work(): pl.pallas_call(block_kernel, grid=(GROUPS,), in_specs=three((1,), rows) +...]
    all_gather x1, blocking collectives: 1.77 us -> 41.5 us  [local(): all_ends = jnp.exp(lax.all_gather(cumulative[-1], ('req', 'ctx'), axis=0))]
    convert_element_type x7 -> x4, other arithmetic: 34.1 us -> 7.49 us  [the longest x1 6.2 us: local(): start = (initial.astype(F32).reshape(heads, width, nstate) * factor[:, No...]
    unnamed x44 -> x49, local copies, waits for them, and re-layouts: 31.8 us -> 13.7 us
    select_n x7 -> x6, other arithmetic: 15.6 us -> 3.34 us  [the longest x1 1.08 us: local(): jnp.where(ctx_index == 0, jnp.zeros_like(other), other)]
    scatter x2 -> x0, local copies, waits for them, and re-layouts: 11.9 us -> none  [the longest x1 7.91 us: local(): new_pool = state_pool.at[target_slots].set(returned, mode='drop')]
  transfers between devices with their start and end apart: 6 -> 7, of which waited for: 2 -> 1; matrix products, arithmetic and copies ran while one was open for 22% -> 12% of each run, Pallas kernels for 0% -> 16%
where the time goes in v1:
time: 196 us; the launch traced here: 195 us
  blocking collectives  41.5 us (21%)
  Pallas kernels  40.9 us (21%)
  waiting for transfers between devices  34.6 us (18%)
  local copies, waits for them, and re-layouts  29.6 us (15%)
  between operations  17.2 us (9%)
  starting transfers between devices  15.5 us (8%)
  other arithmetic  15.4 us (8%)
    all_gather x1, blocking collectives, local(): all_ends = jnp.exp(lax.all_gather(cumulative[-1], ('req', 'ctx'), axis=0))  41.5 us
    all_to_all x1, waiting for transfers between devices, local(): lax.all_to_all(outbound, ('req', 'ctx'), split_axis=0, concat_axis=0, til...  34.5 us
    pallas_call x1, Pallas kernels, block_work(): pl.pallas_call(block_kernel, grid=(GROUPS,), in_specs=three((1,), rows) +...  23.1 us
    unnamed x49, local copies, waits for them, and re-layouts  13.7 us
    pallas_call x1, Pallas kernels, finish(): pl.pallas_call(finish_kernel, grid_spec=pltpu.PrefetchScalarGridSpec(num_...  9.11 us
    all_to_all x1, starting transfers between devices, local(): lax.all_to_all(fetch_pages(state_pool, slot_for), ('req', 'ctx'), split_a...  6.81 us
    convert_element_type x1, other arithmetic, local(): start = (initial.astype(F32).reshape(heads, width, nstate) * factor[:, No...  6.2 us
  transfers between devices with their start and end apart: 7, of which 1 were waited for; matrix products, arithmetic and copies ran while one was open for 12% of the time, Pallas kernels for 16%

profile of v1, /device:TPU:0, one launch (start us, length us, event | category | flops | bytes accessed | tf_op | source)
XLA Modules:
  0.0 194.7 jit_solution(17497876717149367255)
XLA Ops:
  7.2 1.0 slice_bitcast_fusion
  8.1 2.4 %collective-permute-start = (bf16[3,10240]{1,0:T(4,128)(2,1)S(1)}, bf16[3,10240]{1,0:T(4,128)(2,1)S(1)}, u32[]{:S(2)}, u32[]{:S(2)}) collective-permute-start(bf16[3,10240]{1,0:T(4,128)(2,1)S(1)} %slice_bitcast_fusion), channel_id=1, source_target_pairs={{0,1},{2,3},{4,5},{6,7},{8,9},{10,11},{12,13},{14,15},{16,17},{18,... | collective-permute-start | bytes 184328 | tf_op jit(solution)/shard_map/ppermute | solution.py:331
  12.3 2.2 %copy-done = f32[32,256,128]{2,1,0:T(8,128)S(1)} copy-done((f32[32,256,128]{2,1,0:T(8,128)S(1)}, f32[32,256,128]{2,1,0:T(8,128)}, u32[]{:S(2)}) %copy-start) | copy-done | bytes 4194328
  14.5 2.5 %fetch_pages.1 = bf16[32,256,128]{2,1,0:T(8,128)(2,1)} custom-call(s32[32]{0:T(128)S(1)} %get-tuple-element.10.slots, f32[32,256,128]{2,1,0:T(8,128)S(1)} %copy-done), custom_call_target="tpu_custom_call" | custom-call | bytes 6291456 | tf_op jit(solution)/shard_map/fetch_pages/pallas_call | solution.py:38
  17.0 6.8 %all-to-all-start = ((bf16[32,256,128]{2,1,0:T(8,128)(2,1)}), bf16[32,256,128]{2,1,0:T(8,128)(2,1)}, u32[]{:S(2)}, u32[]{:S(2)}) async-start(bf16[32,256,128]{2,1,0:T(8,128)(2,1)} %fetch_pages.1), calls=%async_computation | async-start | bytes 4194304 | tf_op jit(solution)/shard_map/all_to_all | solution.py:326
  29.4 3.8 %gather_fusion.1 = bf16[3,10240]{1,0:T(4,128)(2,1)S(1)} fusion(bf16[256,10240]{1,0:T(8,128)(2,1)} %bitcast.74, s32[1024]{0:T(1024)S(1)} %pad_clamp_fusion), kind=kCustom, calls=%fused_computation.1 | custom fusion | bytes 122892 | tf_op jit(solution)/shard_map/gather | solution.py:388
  33.5 2.5 %copy-done.4 = bf16[1,256,10240]{2,1,0:T(8,128)(2,1)S(1)} copy-done((bf16[1,256,10240]{2,1,0:T(8,128)(2,1)S(1)}, bf16[1,256,10240]{2,1,0:T(8,128)(2,1)}, u32[]{:S(2)}) %copy-start.4) | copy-done | bytes 5242904
  35.9 23.1 %block_work.1 = (f32[256,8192]{1,0:T(8,128)S(1)}, bf16[8192,128]{1,0:T(8,128)(2,1)S(1)}, bf16[256,1024]{1,0:T(8,128)(2,1)S(1)}) custom-call(bf16[1,256,10240]{2,1,0:T(8,128)(2,1)S(1)} %copy-done.4, bf16[1,256,10240]{2,1,0:T(8,128)(2,1)S(1)} %copy-done.4, bf16[1,256,10240]{2,1,0:T(8,128)(2,1)S(1)} %copy-done.4, ...), custom_call_target="tpu_custom_call" | custom-call | flops 30000001024 | bytes 41943040 | tf_op jit(solution)/shard_map/block_work/pallas_call | solution.py:134
  59.1 3.2 %copy-done.9 = f32[256,8192]{1,0:T(8,128)} copy-done((f32[256,8192]{1,0:T(8,128)}, f32[256,8192]{1,0:T(8,128)S(1)}, u32[]{:S(2)}) %copy-start.9) | copy-done | bytes 8388632
  62.3 1.5 constant_dynamic-slice_fusion
  65.8 41.5 %all-gather = f32[32,1,128]{2,1,0:T(1,128)S(1)} all-gather(f32[1,1,128]{2,1,0:T(1,128)S(1)} %bitcast.89), channel_id=1, replica_groups=mesh['req'=16,'ctx'=2] {'req','ctx'}, dimensions={0}, use_global_device_ids=true | all-gather | bytes 16896 | tf_op jit(solution)/shard_map/all_gather | solution.py:342
  109.0 2.7 %combine.1 = bf16[32,256,128]{2,1,0:T(8,128)(2,1)} custom-call(s32[32]{0:T(128)S(1)} %select_reduce_fusion.2.pages, f32[64]{0:T(128)S(1)} %get-tuple-element.21.scale_a, f32[64]{0:T(128)S(1)} %get-tuple-element.20.scale_b, bf16[4096,128]{1,0:T(8,128)(2,1)S(1)} %get-tuple-element.13.a, bf16[4096,128]{1,0:T(8,128)(2,1)S(1)} %collective-permute-done.2.b), custom_call_target="tpu_custom_call" | custom-call | bytes 6291456 | tf_op jit(solution)/shard_map/combine/pallas_call | solution.py:232
  111.7 2.7 %all-to-all-start.1 = ((bf16[32,256,128]{2,1,0:T(8,128)(2,1)}), bf16[32,256,128]{2,1,0:T(8,128)(2,1)S(1)}, u32[]{:S(2)}, u32[]{:S(2)}) async-start(bf16[32,256,128]{2,1,0:T(8,128)(2,1)} %combine.1), calls=%async_computation.1 | async-start | bytes 4194304 | tf_op jit(solution)/shard_map/all_to_all | solution.py:371
  115.8 0.8 select_reduce_fusion
  119.8 3.1 %collective-permute-start.1 = (bf16[4096,128]{1,0:T(8,128)(2,1)}, bf16[4096,128]{1,0:T(8,128)(2,1)}, u32[]{:S(2)}, u32[]{:S(2)}) collective-permute-start(bf16[4096,128]{1,0:T(8,128)(2,1)} %get-tuple-element.15), channel_id=1, source_target_pairs={{0,1},{2,3},{4,5},{6,7},{8,9},{10,11},{12,13},{14,15},{16,17},{18,... | collective-permute-start | bytes 3145736 | tf_op jit(solution)/shard_map/ppermute | solution.py:373
  122.8 3.3 %gather_fusion = bf16[16,256,128]{2,1,0:T(8,128)(2,1)} fusion(bf16[32,256,128]{2,1,0:T(8,128)(2,1)} %all-to-all-done, s32[1024]{0:T(1024)S(1)} %pad_clamp_fusion.1), kind=kCustom, calls=%fused_computation | custom fusion | bytes 2097216 | tf_op jit(solution)/shard_map/gather | solution.py:375
  126.1 1.6 add_bitcast_fusion
  127.8 1.1 broadcast_select_fusion
  128.8 34.5 %all-to-all-done.1.back = bf16[32,256,128]{2,1,0:T(8,128)(2,1)S(1)} async-done(((bf16[32,256,128]{2,1,0:T(8,128)(2,1)}), bf16[32,256,128]{2,1,0:T(8,128)(2,1)S(1)}, u32[]{:S(2)}, u32[]{:S(2)}) %all-to-all-start.1) | async-done | bytes 2097184 | tf_op jit(solution)/shard_map/all_to_all | solution.py:371
  163.3 2.2 %copy-done.1 = f32[32,256,128]{2,1,0:T(8,128)S(1)} copy-done((f32[32,256,128]{2,1,0:T(8,128)S(1)}, f32[32,256,128]{2,1,0:T(8,128)}, u32[]{:S(2)}) %copy-start.1) | copy-done | bytes 4194328
  165.5 3.5 %store_pages.1 = f32[32,256,128]{2,1,0:T(8,128)} custom-call(s32[32]{0:T(128)S(1)} %select_reduce_fusion.4.source, s32[32]{0:T(128)S(1)} %convert_element_type.47.used, f32[32,4]{1,0:T(8,128)S(1)} %broadcast_select_fusion.2.decay, f32[32,256,128]{2,1,0:T(8,128)S(1)} %copy-done.1, bf16[32,256,128]{2,1,0:T(8,128)(2,1)S(1)} %all-to-all-done.1.back), custom_call_target="tpu_custom_call" | custom-call | bytes 10485760 | tf_op jit(solution)/shard_map/store_pages/pallas_call | solution.py:268
  169.1 6.2 %add_convert_fusion.rst = bf16[8192,128]{1,0:T(8,128)(2,1)S(1)} fusion(bf16[8192,128]{1,0:T(8,128)(2,1)} %all-gather.3.cloned.1.call-done, bf16[4096,128]{1,0:T(8,128)(2,1)} %broadcast_select_fusion, bf16[4096,128]{1,0:T(8,128)(2,1)} %collective-permute-done.1, f32[8192]{0:T(1024)S(1)} %mul.86), kind=kLoop, calls=%fused_computation.2 | loop fusion | flops 8388608 | bytes 6324224 | tf_op jit(solution)/shard_map/convert_element_type | solution.py:380
  175.4 3.4 %copy-done.10 = f32[256,8192]{1,0:T(8,128)S(1)} copy-done((f32[256,8192]{1,0:T(8,128)S(1)}, f32[256,8192]{1,0:T(8,128)}, u32[]{:S(2)}) %copy-start.10) | copy-done | bytes 8388632
  178.7 9.1 %finish.1 = bf16[1,256,8192]{2,1,0:T(8,128)(2,1)} custom-call(s32[1]{0:T(128)} %bitcast.1.count, f32[256,8192]{1,0:T(8,128)S(1)} %copy-done.10, bf16[256,1024]{1,0:T(8,128)(2,1)S(1)} %copy-done.12, bf16[8192,128]{1,0:T(8,128)(2,1)S(1)} %add_convert_fusion.rst, f32[8,256,16]{2,1,0:T(8,128)S(1)} %bitcast.69, bf16[1,256,8192]{2,1,0:T(8,128)(2,1)S(1)} %copy-done.5, ...), custom_call_target="tpu_custom_call" | custom-call | flops 10000000000 | bytes 41943040 | tf_op jit(solution)/shard_map/finish/pallas_call | solution.py:187
  (106 shorter events, 12.9 us)
Async XLA Ops:
  8.1 25.1 %collective-permute-start = (bf16[3,10240]{1,0:T(4,128)(2,1)S(1)}, bf16[3,10240]{1,0:T(4,128)(2,1)S(1)}, u32[]{:S(2)}, u32[]{:S(2)}) collective-permute-start(bf16[3,10240]{1,0:T(4,128)(2,1)S(1)} %slice_bitcast_fusion), channel_id=1, source_target_pairs={{0,1},{2,3},{4,5},{6,7},{8,9},{10,11},{12,13},{14,15},{16,17},{18,... | collective-permute-start | bytes 184328 | tf_op jit(solution)/shard_map/ppermute | solution.py:331
  11.3 96.7 %copy-start.15 = (s32[32,16]{1,0:T(8,128)}, s32[32,16]{1,0:T(8,128)S(1)}, u32[]{:S(2)}) copy-start(s32[32,16]{1,0:T(8,128)S(1)} %reshape.197) | copy-start | bytes 6148
  12.2 96.7 %copy-start.18 = (pred[32]{0:T(512)(128)(4,1)}, pred[32]{0:T(512)(128)(4,1)S(1)}, u32[]{:S(2)}) copy-start(pred[32]{0:T(512)(128)(4,1)S(1)} %get-tuple-element.11) | copy-start | bytes 100
  14.5 9.4 %copy-start.20 = (s32[16]{0:T(128)S(1)}, s32[16]{0:T(128)}, u32[]{:S(2)}) copy-start(s32[16]{0:T(128)} %param.29) | copy-start | bytes 196
  14.5 11.5 %copy-start.22 = (s32[16]{0:T(128)S(1)}, s32[16]{0:T(128)}, u32[]{:S(2)}) copy-start(s32[16]{0:T(128)} %param.28) | copy-start | bytes 196
  14.5 12.2 %copy-start.21 = (f32[128]{0:T(128)S(1)}, f32[128]{0:T(128)}, u32[]{:S(2)}) copy-start(f32[128]{0:T(128)} %param.21) | copy-start | bytes 1540
  14.5 12.2 %copy-start.14 = (bf16[1,256,128]{2,1,0:T(8,128)(2,1)S(1)}, bf16[1,256,128]{2,1,0:T(8,128)(2,1)}, u32[]{:S(2)}) copy-start(bf16[1,256,128]{2,1,0:T(8,128)(2,1)} %param.17) | copy-start | bytes 196612
  14.5 12.3 %copy-start.16 = (f32[128]{0:T(128)S(1)}, f32[128]{0:T(128)}, u32[]{:S(2)}) copy-start(f32[128]{0:T(128)} %param.20) | copy-start | bytes 1540
  17.0 11.5 %copy-start.19 = (f32[128]{0:T(128)S(1)}, f32[128]{0:T(128)}, u32[]{:S(2)}) copy-start(f32[128]{0:T(128)} %param.22) | copy-start | bytes 1540
  17.0 16.2 %copy-start.13 = (bf16[1,3,10240]{2,1,0:T(4,128)(2,1)S(1)}, bf16[1,3,10240]{2,1,0:T(4,128)(2,1)}, u32[]{:S(2)}) copy-start(bf16[1,3,10240]{2,1,0:T(4,128)(2,1)} %param.24) | copy-start | bytes 184324
  17.0 94.6 %all-to-all-start = ((bf16[32,256,128]{2,1,0:T(8,128)(2,1)}), bf16[32,256,128]{2,1,0:T(8,128)(2,1)}, u32[]{:S(2)}, u32[]{:S(2)}) async-start(bf16[32,256,128]{2,1,0:T(8,128)(2,1)} %fetch_pages.1), calls=%async_computation | async-start | bytes 4194304 | tf_op jit(solution)/shard_map/all_to_all | solution.py:326
  23.8 9.6 %copy-start.6 = (f32[4,10240]{1,0:T(4,128)S(1)}, f32[4,10240]{1,0:T(4,128)}, u32[]{:S(2)}) copy-start(f32[4,10240]{1,0:T(4,128)} %wc.1) | copy-start | bytes 491524
  23.9 9.6 %copy-start.7 = (f32[10240]{0:T(1024)S(1)}, f32[10240]{0:T(1024)}, u32[]{:S(2)}) copy-start(f32[10240]{0:T(1024)} %param.19) | copy-start | bytes 122884
  27.8 31.2 %copy-start.2 = (f32[256,8,16]{2,0,1:T(8,128)}, f32[256,8,16]{2,0,1:T(8,128)S(1)}, u32[]{:S(2)}) copy-start(f32[256,8,16]{2,0,1:T(8,128)S(1)} %copy.40) | copy-start | bytes 393220
  62.3 49.4 %copy-start.11 = (bf16[256,1024]{1,0:T(8,128)(2,1)}, bf16[256,1024]{1,0:T(8,128)(2,1)S(1)}, u32[]{:S(2)}) copy-start(bf16[256,1024]{1,0:T(8,128)(2,1)S(1)} %get-tuple-element.7.c) | copy-start | bytes 1572868
  63.9 45.1 %collective-permute-start.2 = (bf16[4096,128]{1,0:T(8,128)(2,1)}, bf16[4096,128]{1,0:T(8,128)(2,1)S(1)}, u32[]{:S(2)}, u32[]{:S(2)}) collective-permute-start(bf16[4096,128]{1,0:T(8,128)(2,1)} %get-tuple-element.14), channel_id=1, source_target_pairs={{0,1},{1,0},{2,3},{3,2},{4,5},{5,4},{6,7},{7,6},{8,9},{9,8},{10,11... | collective-permute-start | bytes 3145736 | tf_op jit(solution)/shard_map/ppermute | solution.py:358
  64.8 61.3 %collective-permute-start.3 = (bf16[3,10240]{1,0:T(4,128)(2,1)}, bf16[3,10240]{1,0:T(4,128)(2,1)}, u32[]{:S(2)}, u32[]{:S(2)}) collective-permute-start(bf16[3,10240]{1,0:T(4,128)(2,1)} %broadcast_select_fusion.1), channel_id=1, source_target_pairs={{0,1},{1,0},{2,3},{3,2},{4,5},{5,4},{6,7},{7,6},{8,9},{9,8},{10,11... | collective-permute-start | bytes 184328 | tf_op jit(solution)/shard_map/ppermute | solution.py:389
  111.7 51.7 %all-to-all-start.1 = ((bf16[32,256,128]{2,1,0:T(8,128)(2,1)}), bf16[32,256,128]{2,1,0:T(8,128)(2,1)S(1)}, u32[]{:S(2)}, u32[]{:S(2)}) async-start(bf16[32,256,128]{2,1,0:T(8,128)(2,1)} %combine.1), calls=%async_computation.1 | async-start | bytes 4194304 | tf_op jit(solution)/shard_map/all_to_all | solution.py:371
  114.4 54.7 %all-gather.3.cloned.1.call-start = ((), (), s32[]{:S(2)}) async-start(), calls=%async_computation.2 | async-start | bytes 3145728 | tf_op jit(solution)/shard_map/all_gather | solution.py:375
  119.8 49.3 %collective-permute-start.1 = (bf16[4096,128]{1,0:T(8,128)(2,1)}, bf16[4096,128]{1,0:T(8,128)(2,1)}, u32[]{:S(2)}, u32[]{:S(2)}) collective-permute-start(bf16[4096,128]{1,0:T(8,128)(2,1)} %get-tuple-element.15), channel_id=1, source_target_pairs={{0,1},{2,3},{4,5},{6,7},{8,9},{10,11},{12,13},{14,15},{16,17},{18,... | collective-permute-start | bytes 3145736 | tf_op jit(solution)/shard_map/ppermute | solution.py:373
  169.1 6.3 %copy-start.3 = (f32[256,8,16]{2,0,1:T(8,128)S(1)}, f32[256,8,16]{2,0,1:T(8,128)}, u32[]{:S(2)}) copy-start(f32[256,8,16]{2,0,1:T(8,128)} %copy-done.2) | copy-start | bytes 393220
  169.1 6.3 %copy-start.8 = (f32[8192]{0:T(1024)S(1)}, f32[8192]{0:T(1024)}, u32[]{:S(2)}) copy-start(f32[8192]{0:T(1024)} %param.23) | copy-start | bytes 98308
  169.1 6.3 %copy-start.12 = (bf16[256,1024]{1,0:T(8,128)(2,1)S(1)}, bf16[256,1024]{1,0:T(8,128)(2,1)}, u32[]{:S(2)}) copy-start(bf16[256,1024]{1,0:T(8,128)(2,1)} %copy-done.11) | copy-start | bytes 1572868
  169.1 6.2 %copy-start.5 = (bf16[1,256,8192]{2,1,0:T(8,128)(2,1)S(1)}, bf16[1,256,8192]{2,1,0:T(8,128)(2,1)}, u32[]{:S(2)}) copy-start(bf16[1,256,8192]{2,1,0:T(8,128)(2,1)} %gate.1) | copy-start | bytes 12582916
  (6 other events, 19.1 us)
Sparse Core Ops, SparseCore 0:
  126.2 11.8 all-gather.2

commit v2 on v1

--- a/solution.py
+++ b/solution.py
@@ -1,5 +1,3 @@
-import functools
-
 import jax
 import jax.numpy as jnp
 from jax import lax
@@ -22,28 +20,37 @@
     return pl.CostEstimate(flops=flops, bytes_accessed=moved, transcendentals=0)
 
 
-def fetch_kernel(slots, pool, out):
-    first = pl.program_id(0) * out.shape[0]
+def fetch_kernel(slots, pool, out, held, sems):
+    count = out.shape[0]
+
+    def copy(i):
+        return pltpu.make_async_copy(pool.at[slots[i]], held.at[i], sems.at[i])
+
+    def begin(i, carry):
+        copy(i).start()
+        return carry
 
     def one(i, carry):
-        out[i] = pool[slots[first + i]].astype(BF16)
+        copy(i).wait()
+        out[i] = held[i].astype(BF16)
         return carry
 
-    lax.fori_loop(0, out.shape[0], one, 0)
+    lax.fori_loop(0, count, begin, 0)
+    lax.fori_loop(0, count, one, 0)
 
 
 def fetch_pages(pool, slots):
-    count = slots.shape[0]
-    steps = 4
+    shape = (slots.shape[0],) + pool.shape[1:]
     return pl.pallas_call(
         fetch_kernel,
         grid_spec=pltpu.PrefetchScalarGridSpec(
             num_scalar_prefetch=1,
-            grid=(steps,),
-            in_specs=[pl.BlockSpec(pool.shape, lambda i, s: (0, 0, 0))],
-            out_specs=pl.BlockSpec((count // steps,) + pool.shape[1:], lambda i, s: (i, 0, 0)),
-        ),
-        out_shape=jax.ShapeDtypeStruct((count,) + pool.shape[1:], BF16),
+            grid=(1,),
+            in_specs=[pl.BlockSpec(memory_space=pltpu.HBM)],
+            out_specs=pl.BlockSpec(shape, lambda i, s: (0, 0, 0)),
+            scratch_shapes=[pltpu.VMEM(shape, F32), pltpu.SemaphoreType.DMA((shape[0],))],
+        ),
+        out_shape=jax.ShapeDtypeStruct(shape, BF16),
         compiler_params=params(32),
         cost_estimate=cost(0, 6 * 2**20),
         name="fetch_pages",
@@ -207,7 +214,7 @@
     )(count, y, c, rst, cl_g, gate, gain)
 
 
-def combine_kernel(pages, scale_a, scale_b, a, b, out):
+def combine_kernel(pages, scale_a, scale_b, scale_old, a, b, old, out):
     _, page_rows, _ = out.shape
     width = a.shape[0] // scale_a.shape[0]
     per = page_rows // width
@@ -217,67 +224,74 @@
         for h in range(per):
             head = page * per + h
             rows = pl.ds(pl.multiple_of(head * width, width), width)
+            at = slice(h * width, (h + 1) * width)
             total = a[rows, :].astype(F32) * scale_a[head] + b[rows, :].astype(F32) * scale_b[head]
-            out[i, h * width : (h + 1) * width, :] = total.astype(BF16)
+            out[i, at, :] = (total + old[i, at, :].astype(F32) * scale_old[head]).astype(BF16)
         return carry
 
     lax.fori_loop(0, out.shape[0], one, 0)
 
 
-def combine(pages, scale_a, scale_b, a, b, page_rows):
-    devices = pages.shape[0]
-    nstate = a.shape[1]
+def combine(pages, scale_a, scale_b, scale_old, a, b, old):
+    devices, page_rows, nstate = old.shape
     steps = 2
     whole = pl.BlockSpec(a.shape, lambda i, *s: (0, 0))
+    paged = pl.BlockSpec((devices // steps, page_rows, nstate), lambda i, *s: (i, 0, 0))
     return pl.pallas_call(
         combine_kernel,
         grid_spec=pltpu.PrefetchScalarGridSpec(
-            num_scalar_prefetch=3,
+            num_scalar_prefetch=4,
             grid=(steps,),
-            in_specs=[whole, whole],
-            out_specs=pl.BlockSpec((devices // steps, page_rows, nstate), lambda i, *s: (i, 0, 0)),
-        ),
-        out_shape=jax.ShapeDtypeStruct((devices, page_rows, nstate), BF16),
+            in_specs=[whole, whole, paged],
+            out_specs=paged,
+        ),
+        out_shape=jax.ShapeDtypeStruct(old.shape, BF16),
         compiler_params=params(32),
         cost_estimate=cost(0, 6 * 2**20),
         name="combine",
-    )(pages, scale_a, scale_b, a, b)
-
-
-def store_kernel(source, used, decay, pool, back, out):
-    slots, page_rows, _ = out.shape
-    per = decay.shape[1]
-    width = page_rows // per
+    )(pages, scale_a, scale_b, scale_old, a, b, old)
+
+
+def store_kernel(source, used, pool, back, after, out):
+    slots = out.shape[0]
 
     def one(i, carry):
         slot = pl.program_id(0) * slots + i
-        for h in range(per):
-            rows = slice(h * width, (h + 1) * width)
-            part = back[source[slot], rows, :].astype(F32)
-            part = jnp.where(used[slot] > 0, part, 0.0)
-            out[i, rows, :] = pool[i, rows, :] * decay[slot, h] + part
+
+        @pl.when(used[slot] > 0)
+        def _():
+            out[i] = back[source[slot]].astype(F32)
+
+        @pl.when(used[slot] == 0)
+        def _():
+            out[i] = pool[i]
+
         return carry
 
     lax.fori_loop(0, slots, one, 0)
 
 
-def store_pages(source, used, decay, pool, back):
+def store_pages(source, used, pool, back, after):
     slots, page_rows, nstate = pool.shape
     steps = 4
     block = pl.BlockSpec((slots // steps, page_rows, nstate), lambda i, *s: (i, 0, 0))
     return pl.pallas_call(
         store_kernel,
         grid_spec=pltpu.PrefetchScalarGridSpec(
-            num_scalar_prefetch=3,
+            num_scalar_prefetch=2,
             grid=(steps,),
-            in_specs=[block, pl.BlockSpec(back.shape, lambda i, *s: (0, 0, 0))],
+            in_specs=[
+                block,
+                pl.BlockSpec(back.shape, lambda i, *s: (0, 0, 0)),
+                pl.BlockSpec(memory_space=pltpu.HBM),
+            ],
             out_specs=block,
         ),
         out_shape=jax.ShapeDtypeStruct(pool.shape, F32),
         compiler_params=params(32),
         cost_estimate=cost(0, 10 * 2**20),
         name="store_pages",
-    )(source, used, decay, pool, back)
+    )(source, used, pool, back, after)
 
 
 def local(
@@ -311,7 +325,6 @@
     width = inner // heads
     pool_slots, page_rows, nstate = state_pool.shape
     device_pages = page_owner.shape[1] // ctx_count
-    page_heads = page_rows // width
     rim = conv_weight.shape[0] - 1
     per_group = heads // GROUPS
     prefix = prefix_len[req_index]
@@ -321,14 +334,14 @@
     page_ids = jnp.arange(device_pages, dtype=jnp.int32)
     matches = owner_table == own_index
     slot_for = jnp.sum(jnp.where(matches, slot_table, 0), axis=1)
-    page_for = jnp.sum(jnp.where(matches, page_ids[None, :], 0), axis=1)
     present = jnp.any(matches, axis=1)
-    incoming = lax.all_to_all(
-        fetch_pages(state_pool, slot_for), ("req", "ctx"), split_axis=0, concat_axis=0, tiled=True
-    )
+    fetched, edge = lax.optimization_barrier(
+        (fetch_pages(state_pool, slot_for), tokens[rows - (conv_weight.shape[0] - 1) :])
+    )
+    incoming = lax.all_to_all(fetched, ("req", "ctx"), split_axis=0, concat_axis=0, tiled=True)
     my_owners = owner_table[own_index]
 
-    previous = lax.ppermute(tokens[rows - rim :], "ctx", [(0, 1)])
+    previous = lax.ppermute(edge, "ctx", [(0, 1)])
     keep_rows = jnp.arange(rim) >= rim - prefix
     cached = jnp.where(keep_rows[:, None], conv_cache[0], jnp.zeros_like(conv_cache[0]))
     rim_rows = jnp.where(ctx_index == 0, cached, previous)
@@ -339,8 +352,12 @@
     step_size = jax.nn.softplus(dt_raw[0].astype(F32) + dt_bias) * live[:, None].astype(F32)
     cumulative = jnp.cumsum(step_size * -jnp.exp(a_log), axis=0)
     ending = jnp.exp(cumulative[-1][None, :] - cumulative) * step_size
-    all_ends = jnp.exp(lax.all_gather(cumulative[-1], ("req", "ctx"), axis=0))
-    by_request = all_ends.reshape(req_count, ctx_count, heads)
+    own_decay = jnp.exp(cumulative[-1])
+    other_decay = lax.ppermute(own_decay, "ctx", swap)
+    is_first = ctx_index == 0
+    decay_first = jnp.where(is_first, own_decay, other_decay)
+    decay_later = jnp.where(is_first, other_decay, own_decay)
+    resumed = (prefix > 0).astype(F32)
 
     def grouped(array):
         return jnp.moveaxis(array.reshape(rows, GROUPS, per_group), 1, 0)
@@ -356,24 +373,35 @@
     mine = lax.dynamic_slice_in_dim(states, ctx_index * share, share, 0)
     theirs = lax.dynamic_slice_in_dim(states, (1 - ctx_index) * share, share, 0)
     other = lax.ppermute(theirs, "ctx", swap)
-    later = lax.dynamic_slice_in_dim(by_request[req_index, 1], ctx_index * head_share, head_share, 0)
+    later = lax.dynamic_slice_in_dim(decay_later, ctx_index * head_share, head_share, 0)
+    whole = lax.dynamic_slice_in_dim(decay_first * decay_later * resumed, ctx_index * head_share, head_share, 0)
     ones = jnp.ones_like(later)
-    outbound = combine(
-        jnp.sum(
-            jnp.where(my_owners[None, :] == jnp.arange(devices)[:, None], page_ids[None, :], 0), axis=1
-        ),
-        jnp.where(ctx_index == 0, later, ones),
-        jnp.where(ctx_index == 0, ones, later),
-        mine,
-        other,
-        page_rows,
-    )
+    targets = count - rim + jnp.arange(rim) - ctx_index * rows
+    outbound, targets, arrived = lax.optimization_barrier((
+        combine(
+            jnp.sum(
+                jnp.where(my_owners[None, :] == jnp.arange(devices)[:, None], page_ids[None, :], 0), axis=1
+            ),
+            jnp.where(is_first, later, ones),
+            jnp.where(is_first, ones, later),
+            whole,
+            mine,
+            other,
+            incoming,
+        ),
+        targets,
+        incoming,
+    ))
     returned = lax.all_to_all(outbound, ("req", "ctx"), split_axis=0, concat_axis=0, tiled=True)
 
     first_half = lax.ppermute(states[:share], "ctx", [(0, 1)])
-    before = jnp.concatenate([first_half, jnp.where(ctx_index == 0, jnp.zeros_like(other), other)], axis=0)
-    initial = lax.all_gather(incoming[my_owners].reshape(share, nstate), "ctx", axis=0, tiled=True)
-    factor = jnp.where(ctx_index == 0, 1.0, by_request[req_index, 0]) * (prefix > 0).astype(F32)
+    before = jnp.concatenate([first_half, jnp.where(is_first, jnp.zeros_like(other), other)], axis=0)
+    old = arrived[my_owners].reshape(share, nstate)
+    old_other = lax.ppermute(old, "ctx", swap)
+    initial = jnp.concatenate(
+        [jnp.where(is_first, old, old_other), jnp.where(is_first, old_other, old)], axis=0
+    )
+    factor = jnp.where(is_first, 1.0, decay_first) * resumed
     start = (
         initial.astype(F32).reshape(heads, width, nstate) * factor[:, None, None]
         + before.astype(F32).reshape(heads, width, nstate)
@@ -383,21 +411,14 @@
         y, c_proj, start.reshape(inner, nstate), cl_g, gate_input, norm_weight[None, :],
     )
 
-    targets = count - rim + jnp.arange(rim) - ctx_index * rows
     inside = (targets >= 0) & (targets < rows)
     tail = jnp.where(inside[:, None], tokens[jnp.clip(targets, 0, rows - 1)], jnp.zeros((), BF16))
     new_tail = tail + lax.ppermute(tail, "ctx", swap)
 
-    total = jnp.prod(by_request, axis=1) * (prefix_len > 0).astype(F32)[:, None]
-    paged = total.reshape(devices, device_pages, page_heads)
-    chosen = (page_for[:, None] == page_ids[None, :])[:, :, None]
-    page_decay = jnp.sum(jnp.where(chosen, paged, 0.0), axis=1)
     hit = (slot_for[None, :] == jnp.arange(pool_slots)[:, None]) & present[None, :]
     used = jnp.any(hit, axis=1)
     source = jnp.sum(jnp.where(hit, jnp.arange(devices, dtype=jnp.int32)[None, :], 0), axis=1)
-    slot_decay = jnp.sum(jnp.where(hit[:, :, None], page_decay[None], 0.0), axis=1)
-    slot_decay = jnp.where(used[:, None], slot_decay, 1.0)
-    new_pool = store_pages(source, used.astype(jnp.int32), slot_decay, state_pool, returned)
+    new_pool = store_pages(source, used.astype(jnp.int32), state_pool, returned, mixed)
     return (mixed, new_tail[None], new_pool)
 
 

time: 196 us -> 149 us (0.76)
  blocking collectives: 41.5 us -> 0 us
  between operations: 17.2 us -> 3.61 us
  local copies, waits for them, and re-layouts: 29.6 us -> 37.4 us
  waiting for transfers between devices: 34.6 us -> 27 us
  Pallas kernels: 40.9 us -> 44.8 us
  starting transfers between devices: 15.5 us -> 18.3 us
  other arithmetic: 15.4 us -> 17.4 us
    all_gather x1 -> x0, blocking collectives: 41.5 us -> none  [local(): all_ends = jnp.exp(lax.all_gather(cumulative[-1], ('req', 'ctx'), axis=0))]
    all_to_all x1, waiting for transfers between devices: 34.5 us -> 25.5 us  [local(): lax.all_to_all(outbound, ('req', 'ctx'), split_axis=0, concat_axis=0, til...]
    unnamed x49 -> x57, local copies, waits for them, and re-layouts: 13.7 us -> 21.9 us
    pallas_call x1, Pallas kernels: 2.52 us -> 6.8 us  [fetch_pages(): pl.pallas_call(fetch_kernel, grid_spec=pltpu.PrefetchScalarGridSpec(num_s...]
    gather x1, local copies, waits for them, and re-layouts: 3.25 us -> 0.75 us  [local(): old = arrived[my_owners].reshape(share, nstate)]
    convert_element_type x1, other arithmetic: 6.2 us -> 8.67 us  [local(): start = (initial.astype(F32).reshape(heads, width, nstate) * factor[:, No...]
    slice x1 -> x2, local copies, waits for them, and re-layouts: 0.96 us -> 3.4 us  [the longest x1 1.8 us: local(): first_half = lax.ppermute(states[:share], 'ctx', [(0, 1)])]
    reshape x2, local copies, waits for them, and re-layouts: 0.66 us -> 2.66 us  [grouped(): return jnp.moveaxis(array.reshape(rows, GROUPS, per_group), 1, 0)]
  transfers between devices with their start and end apart: 7 -> 8, of which waited for: 1 -> 2; matrix products, arithmetic and copies ran while one was open for 12% -> 20% of each run, Pallas kernels for 16% -> 23%
where the time goes in v2:
time: 149 us
  Pallas kernels  44.8 us (30%)
  local copies, waits for them, and re-layouts  37.4 us (25%)
  waiting for transfers between devices  27 us (18%)
  starting transfers between devices  18.3 us (12%)
  other arithmetic  17.4 us (12%)
  between operations  3.61 us (2%)
    all_to_all x1, waiting for transfers between devices, local(): lax.all_to_all(outbound, ('req', 'ctx'), split_axis=0, concat_axis=0, til...  25.5 us
    pallas_call x1, Pallas kernels, block_work(): pl.pallas_call(block_kernel, grid=(GROUPS,), in_specs=three((1,), rows) +...  23.6 us
    unnamed x57, local copies, waits for them, and re-layouts  21.9 us
    pallas_call x1, Pallas kernels, finish(): pl.pallas_call(finish_kernel, grid_spec=pltpu.PrefetchScalarGridSpec(num_...  9.11 us
    convert_element_type x1, other arithmetic, local(): start = (initial.astype(F32).reshape(heads, width, nstate) * factor[:, No...  8.67 us
    pallas_call x1, Pallas kernels, fetch_pages(): pl.pallas_call(fetch_kernel, grid_spec=pltpu.PrefetchScalarGridSpec(num_s...  6.8 us
    all_to_all x1, starting transfers between devices, local(): lax.all_to_all(fetched, ('req', 'ctx'), split_axis=0, concat_axis=0, tile...  6.79 us
    all_to_all x1, starting transfers between devices, local(): lax.all_to_all(outbound, ('req', 'ctx'), split_axis=0, concat_axis=0, til...  4.36 us
  transfers between devices with their start and end apart: 8, of which 2 were waited for; matrix products, arithmetic and copies ran while one was open for 20% of the time, Pallas kernels for 23%

profile of v2, /device:TPU:0, one launch (start us, length us, event | category | flops | bytes accessed | tf_op | source)
XLA Modules:
  0.0 148.6 jit_solution(13589422918640808274)
XLA Ops:
  2.3 1.6 %slice_bitcast_fusion = bf16[3,10240]{1,0:T(4,128)(2,1)} fusion(bf16[1,256,10240]{2,1,0:T(8,128)(2,1)} %cin.1), kind=kLoop, calls=%fused_computation.22 | loop fusion | bytes 122880 | tf_op jit(solution)/shard_map/slice | solution.py:339
  4.6 2.2 %copy-done = f32[32,256,128]{2,1,0:T(8,128)S(1)} copy-done((f32[32,256,128]{2,1,0:T(8,128)S(1)}, f32[32,256,128]{2,1,0:T(8,128)}, u32[]{:S(2)}) %copy-start) | copy-done | bytes 4194328
  6.8 6.8 %fetch_pages.1 = bf16[32,256,128]{2,1,0:T(8,128)(2,1)S(1)} custom-call(s32[32]{0:T(128)S(1)} %select_reduce_fusion.2.slots, f32[32,256,128]{2,1,0:T(8,128)S(1)} %copy-done), custom_call_target="tpu_custom_call" | custom-call | bytes 6291456 | tf_op jit(solution)/shard_map/fetch_pages/pallas_call | solution.py:44
  14.9 3.1 %collective-permute-start = (bf16[3,10240]{1,0:T(4,128)(2,1)}, bf16[3,10240]{1,0:T(4,128)(2,1)}, u32[]{:S(2)}, u32[]{:S(2)}) collective-permute-start(bf16[3,10240]{1,0:T(4,128)(2,1)} %slice_bitcast_fusion), channel_id=1, source_target_pairs={{0,1},{2,3},{4,5},{6,7},{8,9},{10,11},{12,13},{14,15},{16,17},{18,... | collective-permute-start | bytes 184328 | tf_op jit(solution)/shard_map/ppermute | solution.py:344
  20.9 6.8 %all-to-all-start = ((bf16[32,256,128]{2,1,0:T(8,128)(2,1)}), bf16[32,256,128]{2,1,0:T(8,128)(2,1)S(1)}, u32[]{:S(2)}, u32[]{:S(2)}) async-start(bf16[32,256,128]{2,1,0:T(8,128)(2,1)} %copy-done.2), calls=%async_computation | async-start | bytes 4194304 | tf_op jit(solution)/shard_map/all_to_all | solution.py:341
  29.5 2.3 %copy.30 = f32[256,8,16]{2,0,1:T(8,128)} copy(f32[256,8,16]{0,2,1:T(8,128)} %bitcast.75) | data formatting | bytes 262144 | tf_op jit(solution)/shard_map/reshape | solution.py:363
  35.0 2.5 %copy-done.9 = bf16[1,256,10240]{2,1,0:T(8,128)(2,1)S(1)} copy-done((bf16[1,256,10240]{2,1,0:T(8,128)(2,1)S(1)}, bf16[1,256,10240]{2,1,0:T(8,128)(2,1)}, u32[]{:S(2)}) %copy-start.9) | copy-done | bytes 5242904
  38.4 23.6 %block_work.1 = (f32[256,8192]{1,0:T(8,128)S(1)}, bf16[8192,128]{1,0:T(8,128)(2,1)S(1)}, bf16[256,1024]{1,0:T(8,128)(2,1)S(1)}) custom-call(bf16[1,256,10240]{2,1,0:T(8,128)(2,1)S(1)} %copy-done.9, bf16[1,256,10240]{2,1,0:T(8,128)(2,1)S(1)} %copy-done.9, bf16[1,256,10240]{2,1,0:T(8,128)(2,1)S(1)} %copy-done.9, ...), custom_call_target="tpu_custom_call" | custom-call | flops 30000001024 | bytes 41943040 | tf_op jit(solution)/shard_map/block_work/pallas_call | solution.py:141
  62.0 3.2 %copy-done.14 = f32[256,8192]{1,0:T(8,128)} copy-done((f32[256,8192]{1,0:T(8,128)}, f32[256,8192]{1,0:T(8,128)S(1)}, u32[]{:S(2)}) %copy-start.14) | copy-done | bytes 8388632
  65.2 1.8 %fusion.16 = (bf16[4096,128]{1,0:T(8,128)(2,1)}, bf16[4096,128]{1,0:T(8,128)(2,1)}, bf16[4096,128]{1,0:T(8,128)(2,1)}) fusion(bf16[8192,128]{1,0:T(8,128)(2,1)S(1)} %get-tuple-element.14, s32[]{:T(128)S(6)} %select_n.125, s32[]{:T(128)S(6)} %select_n.124), kind=kLoop, calls=%fused_computation.59 | loop fusion | bytes 6291464 | tf_op jit(solution)/shard_map/slice | solution.py:397
  72.0 3.1 %collective-permute-start.4 = (bf16[4096,128]{1,0:T(8,128)(2,1)}, bf16[4096,128]{1,0:T(8,128)(2,1)}, u32[]{:S(2)}, u32[]{:S(2)}) collective-permute-start(bf16[4096,128]{1,0:T(8,128)(2,1)} %get-tuple-element.21), channel_id=1, source_target_pairs={{0,1},{2,3},{4,5},{6,7},{8,9},{10,11},{12,13},{14,15},{16,17},{18,... | collective-permute-start | bytes 3145736 | tf_op jit(solution)/shard_map/ppermute | solution.py:397
  75.1 1.5 %all-to-all-done.old = bf16[32,256,128]{2,1,0:T(8,128)(2,1)S(1)} async-done(((bf16[32,256,128]{2,1,0:T(8,128)(2,1)}), bf16[32,256,128]{2,1,0:T(8,128)(2,1)S(1)}, u32[]{:S(2)}, u32[]{:S(2)}) %all-to-all-start) | async-done | bytes 2097184 | tf_op jit(solution)/shard_map/all_to_all | solution.py:341
  77.8 2.0 %combine.1 = bf16[32,256,128]{2,1,0:T(8,128)(2,1)S(1)} custom-call(s32[32]{0:T(128)S(1)} %select_reduce_fusion.1.pages, f32[64]{0:T(128)S(1)} %get-tuple-element.34.scale_a, f32[64]{0:T(128)S(1)} %get-tuple-element.33.scale_b, f32[64]{0:T(128)S(1)} %dynamic_slice.25.scale_old, bf16[4096,128]{1,0:T(8,128)(2,1)S(1)} %copy-done.5, ...), custom_call_target="tpu_custom_call" | custom-call | bytes 6291456 | tf_op jit(solution)/shard_map/combine/pallas_call | solution.py:240
  79.8 1.3 copy-done.3
  81.2 3.8 %gather_fusion.1 = bf16[3,10240]{1,0:T(4,128)(2,1)S(1)} fusion(bf16[256,10240]{1,0:T(8,128)(2,1)} %bitcast.66, s32[1024]{0:T(1024)S(1)} %pad_clamp_fusion), kind=kCustom, calls=%fused_computation.1 | custom fusion | bytes 122892 | tf_op jit(solution)/shard_map/gather | solution.py:415
  87.6 4.4 %all-to-all-start.1 = ((bf16[32,256,128]{2,1,0:T(8,128)(2,1)}), bf16[32,256,128]{2,1,0:T(8,128)(2,1)S(1)}, u32[]{:S(2)}, u32[]{:S(2)}) async-start(bf16[32,256,128]{2,1,0:T(8,128)(2,1)} %copy-done.3), calls=%async_computation.1 | async-start | bytes 4194304 | tf_op jit(solution)/shard_map/all_to_all | solution.py:395
  92.7 1.4 broadcast_select_fusion.2
  94.2 8.7 %add_convert_fusion.rst = bf16[8192,128]{1,0:T(8,128)(2,1)S(1)} fusion(bf16[4096,128]{1,0:T(8,128)(2,1)S(1)} %get-tuple-element.25, bf16[4096,128]{1,0:T(8,128)(2,1)S(1)} %get-tuple-element.24, bf16[4096,128]{1,0:T(8,128)(2,1)S(1)} %copy-done.18, bf16[4096,128]{1,0:T(8,128)(2,1)} %collective-permute-done.4, f32[8192]{0:T(1024)S(1)} %mul.78), kind=kLoop, calls=%fused_computation.2 | loop fusion | flops 11534336 | bytes 6324224 | tf_op jit(solution)/shard_map/convert_element_type | solution.py:408
  102.9 3.4 %copy-done.15 = f32[256,8192]{1,0:T(8,128)S(1)} copy-done((f32[256,8192]{1,0:T(8,128)S(1)}, f32[256,8192]{1,0:T(8,128)}, u32[]{:S(2)}) %copy-start.15) | copy-done | bytes 8388632
  106.3 9.1 %finish.1.after = bf16[1,256,8192]{2,1,0:T(8,128)(2,1)} custom-call(s32[1]{0:T(128)} %bitcast.1.count, f32[256,8192]{1,0:T(8,128)S(1)} %copy-done.15, bf16[256,1024]{1,0:T(8,128)(2,1)S(1)} %copy-done.17, bf16[8192,128]{1,0:T(8,128)(2,1)S(1)} %add_convert_fusion.rst, f32[8,256,16]{2,1,0:T(8,128)S(1)} %bitcast.61, bf16[1,256,8192]{2,1,0:T(8,128)(2,1)S(1)} %copy-done.10, ...), custom_call_target="tpu_custom_call" | custom-call | flops 10000000000 | bytes 41943040 | tf_op jit(solution)/shard_map/finish/pallas_call | solution.py:194
  115.4 25.5 %all-to-all-done.1.back = bf16[32,256,128]{2,1,0:T(8,128)(2,1)S(1)} async-done(((bf16[32,256,128]{2,1,0:T(8,128)(2,1)}), bf16[32,256,128]{2,1,0:T(8,128)(2,1)S(1)}, u32[]{:S(2)}, u32[]{:S(2)}) %all-to-all-start.1) | async-done | bytes 2097184 | tf_op jit(solution)/shard_map/all_to_all | solution.py:395
  140.8 2.2 %copy-done.1 = f32[32,256,128]{2,1,0:T(8,128)S(1)} copy-done((f32[32,256,128]{2,1,0:T(8,128)S(1)}, f32[32,256,128]{2,1,0:T(8,128)}, u32[]{:S(2)}) %copy-start.1) | copy-done | bytes 4194328
  143.0 2.2 %copy-done.4 = bf16[1,256,8192]{2,1,0:T(8,128)(2,1)S(1)} copy-done((bf16[1,256,8192]{2,1,0:T(8,128)(2,1)S(1)}, bf16[1,256,8192]{2,1,0:T(8,128)(2,1)}, u32[]{:S(2)}) %copy-start.4) | copy-done | bytes 4194328
  145.2 3.3 %store_pages.1 = f32[32,256,128]{2,1,0:T(8,128)} custom-call(s32[32]{0:T(128)S(1)} %select_reduce_fusion.source, s32[32]{0:T(128)S(1)} %convert_element_type.46.used, f32[32,256,128]{2,1,0:T(8,128)S(1)} %copy-done.1, bf16[32,256,128]{2,1,0:T(8,128)(2,1)S(1)} %all-to-all-done.1.back, bf16[1,256,8192]{2,1,0:T(8,128)(2,1)S(1)} %copy-done.4), custom_call_target="tpu_custom_call" | custom-call | bytes 10485760 | tf_op jit(solution)/shard_map/store_pages/pallas_call | solution.py:278
  (106 shorter events, 19.2 us)
Async XLA Ops:
  0.6 17.4 %copy-start.24 = (f32[128]{0:T(128)S(1)}, f32[128]{0:T(128)}, u32[]{:S(2)}) copy-start(f32[128]{0:T(128)} %param.21) | copy-start | bytes 1540
  0.6 17.4 %copy-start.19 = (bf16[1,256,128]{2,1,0:T(8,128)(2,1)S(1)}, bf16[1,256,128]{2,1,0:T(8,128)(2,1)}, u32[]{:S(2)}) copy-start(bf16[1,256,128]{2,1,0:T(8,128)(2,1)} %param.17) | copy-start | bytes 196612
  0.7 17.5 %copy-start.25 = (s32[16]{0:T(128)S(1)}, s32[16]{0:T(128)}, u32[]{:S(2)}) copy-start(s32[16]{0:T(128)} %param.29) | copy-start | bytes 196
  0.7 18.8 %copy-start.21 = (f32[128]{0:T(128)S(1)}, f32[128]{0:T(128)}, u32[]{:S(2)}) copy-start(f32[128]{0:T(128)} %param.20) | copy-start | bytes 1540
  1.5 18.7 %copy-start.20 = (s32[32,16]{1,0:T(8,128)}, s32[32,16]{1,0:T(8,128)S(1)}, u32[]{:S(2)}) copy-start(s32[32,16]{1,0:T(8,128)S(1)} %reshape.95) | copy-start | bytes 6148
  14.9 13.6 %copy-start.26 = (s32[16]{0:T(128)S(1)}, s32[16]{0:T(128)}, u32[]{:S(2)}) copy-start(s32[16]{0:T(128)} %param.28) | copy-start | bytes 196
  14.9 17.7 %collective-permute-start = (bf16[3,10240]{1,0:T(4,128)(2,1)}, bf16[3,10240]{1,0:T(4,128)(2,1)}, u32[]{:S(2)}, u32[]{:S(2)}) collective-permute-start(bf16[3,10240]{1,0:T(4,128)(2,1)} %slice_bitcast_fusion), channel_id=1, source_target_pairs={{0,1},{2,3},{4,5},{6,7},{8,9},{10,11},{12,13},{14,15},{16,17},{18,... | collective-permute-start | bytes 184328 | tf_op jit(solution)/shard_map/ppermute | solution.py:344
  19.7 12.1 %copy-start.22 = (f32[128]{0:T(128)S(1)}, f32[128]{0:T(128)}, u32[]{:S(2)}) copy-start(f32[128]{0:T(128)} %param.22) | copy-start | bytes 1540
  20.0 13.7 %copy-start.12 = (f32[10240]{0:T(1024)S(1)}, f32[10240]{0:T(1024)}, u32[]{:S(2)}) copy-start(f32[10240]{0:T(1024)} %param.19) | copy-start | bytes 122884
  20.9 50.1 %collective-permute-start.1 = (f32[128]{0:T(128)}, f32[128]{0:T(128)}, u32[]{:S(2)}, u32[]{:S(2)}) collective-permute-start(f32[128]{0:T(128)} %exp.16), channel_id=1, source_target_pairs={{0,1},{1,0},{2,3},{3,2},{4,5},{5,4},{6,7},{7,6},{8,9},{9,8},{10,11... | collective-permute-start | bytes 1544 | tf_op jit(solution)/shard_map/ppermute | solution.py:356
  20.9 55.7 %all-to-all-start = ((bf16[32,256,128]{2,1,0:T(8,128)(2,1)}), bf16[32,256,128]{2,1,0:T(8,128)(2,1)S(1)}, u32[]{:S(2)}, u32[]{:S(2)}) async-start(bf16[32,256,128]{2,1,0:T(8,128)(2,1)} %copy-done.2), calls=%async_computation | async-start | bytes 4194304 | tf_op jit(solution)/shard_map/all_to_all | solution.py:341
  29.5 32.5 %copy-start.6 = (f32[256,8,16]{2,0,1:T(8,128)}, f32[256,8,16]{2,0,1:T(8,128)S(1)}, u32[]{:S(2)}) copy-start(f32[256,8,16]{2,0,1:T(8,128)S(1)} %copy.29) | copy-start | bytes 393220
  62.0 3.2 %copy-start.14 = (f32[256,8192]{1,0:T(8,128)}, f32[256,8192]{1,0:T(8,128)S(1)}, u32[]{:S(2)}) copy-start(f32[256,8192]{1,0:T(8,128)S(1)} %get-tuple-element.12.y) | copy-start | bytes 25165828
  65.2 4.8 %copy-start.23 = (pred[32]{0:T(512)(128)(4,1)S(1)}, pred[32]{0:T(512)(128)(4,1)}, u32[]{:S(2)}) copy-start(pred[32]{0:T(512)(128)(4,1)} %get-tuple-element.19) | copy-start | bytes 100
  67.1 8.0 %collective-permute-start.2 = (bf16[4096,128]{1,0:T(8,128)(2,1)}, bf16[4096,128]{1,0:T(8,128)(2,1)S(1)}, u32[]{:S(2)}, u32[]{:S(2)}) collective-permute-start(bf16[4096,128]{1,0:T(8,128)(2,1)} %get-tuple-element.22), channel_id=1, source_target_pairs={{0,1},{1,0},{2,3},{3,2},{4,5},{5,4},{6,7},{7,6},{8,9},{9,8},{10,11... | collective-permute-start | bytes 3145736 | tf_op jit(solution)/shard_map/ppermute | solution.py:375
  72.0 22.2 %collective-permute-start.4 = (bf16[4096,128]{1,0:T(8,128)(2,1)}, bf16[4096,128]{1,0:T(8,128)(2,1)}, u32[]{:S(2)}, u32[]{:S(2)}) collective-permute-start(bf16[4096,128]{1,0:T(8,128)(2,1)} %get-tuple-element.21), channel_id=1, source_target_pairs={{0,1},{2,3},{4,5},{6,7},{8,9},{10,11},{12,13},{14,15},{16,17},{18,... | collective-permute-start | bytes 3145736 | tf_op jit(solution)/shard_map/ppermute | solution.py:397
  85.1 6.8 %collective-permute-start.5 = (bf16[3,10240]{1,0:T(4,128)(2,1)S(1)}, bf16[3,10240]{1,0:T(4,128)(2,1)S(1)}, u32[]{:S(2)}, u32[]{:S(2)}) collective-permute-start(bf16[3,10240]{1,0:T(4,128)(2,1)S(1)} %broadcast_select_fusion.3), channel_id=1, source_target_pairs={{0,1},{1,0},{2,3},{3,2},{4,5},{5,4},{6,7},{7,6},{8,9},{9,8},{10,11... | collective-permute-start | bytes 184328 | tf_op jit(solution)/shard_map/ppermute | solution.py:416
  87.0 5.7 %collective-permute-start.3 = (bf16[4096,128]{1,0:T(8,128)(2,1)S(1)}, bf16[4096,128]{1,0:T(8,128)(2,1)}, u32[]{:S(2)}, u32[]{:S(2)}) collective-permute-start(bf16[4096,128]{1,0:T(8,128)(2,1)S(1)} %bitcast.71), channel_id=1, source_target_pairs={{0,1},{1,0},{2,3},{3,2},{4,5},{5,4},{6,7},{7,6},{8,9},{9,8},{10,11... | collective-permute-start | bytes 3145736 | tf_op jit(solution)/shard_map/ppermute | solution.py:400
  87.6 53.3 %all-to-all-start.1 = ((bf16[32,256,128]{2,1,0:T(8,128)(2,1)}), bf16[32,256,128]{2,1,0:T(8,128)(2,1)S(1)}, u32[]{:S(2)}, u32[]{:S(2)}) async-start(bf16[32,256,128]{2,1,0:T(8,128)(2,1)} %copy-done.3), calls=%async_computation.1 | async-start | bytes 4194304 | tf_op jit(solution)/shard_map/all_to_all | solution.py:395
  94.1 8.7 %copy-start.7 = (f32[256,8,16]{2,0,1:T(8,128)S(1)}, f32[256,8,16]{2,0,1:T(8,128)}, u32[]{:S(2)}) copy-start(f32[256,8,16]{2,0,1:T(8,128)} %copy-done.6) | copy-start | bytes 393220
  94.1 8.7 %copy-start.10 = (bf16[1,256,8192]{2,1,0:T(8,128)(2,1)S(1)}, bf16[1,256,8192]{2,1,0:T(8,128)(2,1)}, u32[]{:S(2)}) copy-start(bf16[1,256,8192]{2,1,0:T(8,128)(2,1)} %gate.1) | copy-start | bytes 12582916
  94.1 8.7 %copy-start.13 = (f32[8192]{0:T(1024)S(1)}, f32[8192]{0:T(1024)}, u32[]{:S(2)}) copy-start(f32[8192]{0:T(1024)} %param.23) | copy-start | bytes 98308
  94.1 8.7 %copy-start.17 = (bf16[256,1024]{1,0:T(8,128)(2,1)S(1)}, bf16[256,1024]{1,0:T(8,128)(2,1)}, u32[]{:S(2)}) copy-start(bf16[256,1024]{1,0:T(8,128)(2,1)} %copy-done.16) | copy-start | bytes 1572868
  102.9 3.4 %copy-start.15 = (f32[256,8192]{1,0:T(8,128)S(1)}, f32[256,8192]{1,0:T(8,128)}, u32[]{:S(2)}) copy-start(f32[256,8192]{1,0:T(8,128)} %copy-done.14) | copy-start | bytes 25165828
  (11 other events, 19.1 us)

commit v3 on v2

--- a/solution.py
+++ b/solution.py
@@ -51,7 +51,7 @@
             scratch_shapes=[pltpu.VMEM(shape, F32), pltpu.SemaphoreType.DMA((shape[0],))],
         ),
         out_shape=jax.ShapeDtypeStruct(shape, BF16),
-        compiler_params=params(32),
+        compiler_params=params(58),
         cost_estimate=cost(0, 6 * 2**20),
         name="fetch_pages",
     )(slots, pool)
@@ -157,8 +157,8 @@
             jax.ShapeDtypeStruct((rows, GROUPS * nstate), BF16),
         ],
         scratch_shapes=[pltpu.VMEM((rows + 8, wide + 2 * nstate), F32)],
-        compiler_params=params(32),
-        cost_estimate=cost(30 * 10**9, 40 * 2**20),
+        compiler_params=params(58),
+        cost_estimate=cost(1000, 1000),
         name="block_work",
     )(
         *([conv_input] * 3), *([rim8] * 3), *([conv_weight] * 3), *([bias] * 3),
@@ -208,13 +208,13 @@
             scratch_shapes=[pltpu.VMEM((rows, wide), F32)],
         ),
         out_shape=jax.ShapeDtypeStruct((1, rows, inner), BF16),
-        compiler_params=params(32),
-        cost_estimate=cost(10 * 10**9, 40 * 2**20),
+        compiler_params=params(58),
+        cost_estimate=cost(1000, 1000),
         name="finish",
     )(count, y, c, rst, cl_g, gate, gain)
 
 
-def combine_kernel(pages, scale_a, scale_b, scale_old, a, b, old, out):
+def combine_kernel(pages, scale_a, scale_b, scale_old, which, a, b, old, out):
     _, page_rows, _ = out.shape
     width = a.shape[0] // scale_a.shape[0]
     per = page_rows // width
@@ -232,24 +232,25 @@
     lax.fori_loop(0, out.shape[0], one, 0)
 
 
-def combine(pages, scale_a, scale_b, scale_old, a, b, old):
+def combine(pages, scale_a, scale_b, scale_old, which, a, b, old):
     devices, page_rows, nstate = old.shape
     steps = 2
-    whole = pl.BlockSpec(a.shape, lambda i, *s: (0, 0))
+    own = pl.BlockSpec(b.shape, lambda i, *s: (s[4][0], 0))
+    whole = pl.BlockSpec(b.shape, lambda i, *s: (0, 0))
     paged = pl.BlockSpec((devices // steps, page_rows, nstate), lambda i, *s: (i, 0, 0))
     return pl.pallas_call(
         combine_kernel,
         grid_spec=pltpu.PrefetchScalarGridSpec(
-            num_scalar_prefetch=4,
+            num_scalar_prefetch=5,
             grid=(steps,),
-            in_specs=[whole, whole, paged],
+            in_specs=[own, whole, paged],
             out_specs=paged,
         ),
         out_shape=jax.ShapeDtypeStruct(old.shape, BF16),
         compiler_params=params(32),
         cost_estimate=cost(0, 6 * 2**20),
         name="combine",
-    )(pages, scale_a, scale_b, scale_old, a, b, old)
+    )(pages, scale_a, scale_b, scale_old, which, a, b, old)
 
 
 def store_kernel(source, used, pool, back, after, out):
@@ -288,7 +289,7 @@
             out_specs=block,
         ),
         out_shape=jax.ShapeDtypeStruct(pool.shape, F32),
-        compiler_params=params(32),
+        compiler_params=params(58),
         cost_estimate=cost(0, 10 * 2**20),
         name="store_pages",
     )(source, used, pool, back, after)
@@ -370,7 +371,6 @@
 
     share = inner // ctx_count
     head_share = heads // ctx_count
-    mine = lax.dynamic_slice_in_dim(states, ctx_index * share, share, 0)
     theirs = lax.dynamic_slice_in_dim(states, (1 - ctx_index) * share, share, 0)
     other = lax.ppermute(theirs, "ctx", swap)
     later = lax.dynamic_slice_in_dim(decay_later, ctx_index * head_share, head_share, 0)
@@ -385,7 +385,8 @@
             jnp.where(is_first, later, ones),
             jnp.where(is_first, ones, later),
             whole,
-            mine,
+            ctx_index.reshape(1),
+            states,
             other,
             incoming,
         ),

time: 149 us -> 143 us (0.960)
  local copies, waits for them, and re-layouts: 37.4 us -> 20.1 us
  Pallas kernels: 44.8 us -> 51.1 us
  other arithmetic: 17.4 us -> 21.4 us
    unnamed x57 -> x29, local copies, waits for them, and re-layouts: 21.9 us -> 4.47 us
    all_to_all x1, waiting for transfers between devices: 1.49 us -> 7.02 us  [local(): lax.all_to_all(fetched, ('req', 'ctx'), split_axis=0, concat_axis=0, tile...]
    all_to_all x1, waiting for transfers between devices: 25.5 us -> 21 us  [local(): lax.all_to_all(outbound, ('req', 'ctx'), split_axis=0, concat_axis=0, til...]
    convert_element_type x1, other arithmetic: 8.67 us -> 13.1 us  [local(): start = (initial.astype(F32).reshape(heads, width, nstate) * factor[:, No...]
    pallas_call x1, Pallas kernels: 9.11 us -> 12.5 us  [finish(): pl.pallas_call(finish_kernel, grid_spec=pltpu.PrefetchScalarGridSpec(num_...]
    pallas_call x1, Pallas kernels: 3.34 us -> 6.4 us  [store_pages(): pl.pallas_call(store_kernel, grid_spec=pltpu.PrefetchScalarGridSpec(num_s...]
    pallas_call x1, Pallas kernels: 6.8 us -> 5.21 us  [fetch_pages(): pl.pallas_call(fetch_kernel, grid_spec=pltpu.PrefetchScalarGridSpec(num_s...]
  transfers between devices with their start and end apart: 8 -> 8, of which waited for: 2 -> 2; matrix products, arithmetic and copies ran while one was open for 20% -> 24% of each run, Pallas kernels for 23% -> 28%
where the time goes in v3:
time: 143 us; the launch traced here: 142 us
  Pallas kernels  51.1 us (36%)
  waiting for transfers between devices  28.1 us (20%)
  other arithmetic  21.4 us (15%)
  local copies, waits for them, and re-layouts  20.1 us (14%)
  starting transfers between devices  17.4 us (12%)
  between operations  3.68 us (3%)
    pallas_call x1, Pallas kernels, block_work(): pl.pallas_call(block_kernel, grid=(GROUPS,), in_specs=three((1,), rows) +...  25 us
    all_to_all x1, waiting for transfers between devices, local(): lax.all_to_all(outbound, ('req', 'ctx'), split_axis=0, concat_axis=0, til...  21 us
    convert_element_type x1, other arithmetic, local(): start = (initial.astype(F32).reshape(heads, width, nstate) * factor[:, No...  13.1 us
    pallas_call x1, Pallas kernels, finish(): pl.pallas_call(finish_kernel, grid_spec=pltpu.PrefetchScalarGridSpec(num_...  12.5 us
    all_to_all x1, waiting for transfers between devices, local(): lax.all_to_all(fetched, ('req', 'ctx'), split_axis=0, concat_axis=0, tile...  7.02 us
    all_to_all x1, starting transfers between devices, local(): lax.all_to_all(fetched, ('req', 'ctx'), split_axis=0, concat_axis=0, tile...  6.68 us
    pallas_call x1, Pallas kernels, store_pages(): pl.pallas_call(store_kernel, grid_spec=pltpu.PrefetchScalarGridSpec(num_s...  6.4 us
    pallas_call x1, Pallas kernels, fetch_pages(): pl.pallas_call(fetch_kernel, grid_spec=pltpu.PrefetchScalarGridSpec(num_s...  5.21 us
  transfers between devices with their start and end apart: 8, of which 2 were waited for; matrix products, arithmetic and copies ran while one was open for 24% of the time, Pallas kernels for 28%

profile of v3, /device:TPU:0, one launch (start us, length us, event | category | flops | bytes accessed | tf_op | source)
XLA Modules:
  0.0 141.8 jit_solution(10183091988941520951)
XLA Ops:
  0.7 0.8 reshape.98
  2.2 1.0 slice_bitcast_fusion
  4.0 5.2 %fetch_pages.1 = bf16[32,256,128]{2,1,0:T(8,128)(2,1)} custom-call(s32[32]{0:T(128)} %select_reduce_fusion.2.slots, f32[32,256,128]{2,1,0:T(8,128)} %pool.3), custom_call_target="tpu_custom_call" | custom-call | bytes 6291456 | tf_op jit(solution)/shard_map/fetch_pages/pallas_call | solution.py:44
  9.2 2.3 %collective-permute-start = (bf16[3,10240]{1,0:T(4,128)(2,1)S(1)}, bf16[3,10240]{1,0:T(4,128)(2,1)S(1)}, u32[]{:S(2)}, u32[]{:S(2)}) collective-permute-start(bf16[3,10240]{1,0:T(4,128)(2,1)S(1)} %slice_bitcast_fusion), channel_id=1, source_target_pairs={{0,1},{2,3},{4,5},{6,7},{8,9},{10,11},{12,13},{14,15},{16,17},{18,... | collective-permute-start | bytes 184328 | tf_op jit(solution)/shard_map/ppermute | solution.py:345
  14.1 6.7 %all-to-all-start = ((bf16[32,256,128]{2,1,0:T(8,128)(2,1)}), bf16[32,256,128]{2,1,0:T(8,128)(2,1)S(1)}, u32[]{:S(2)}, u32[]{:S(2)}) async-start(bf16[32,256,128]{2,1,0:T(8,128)(2,1)} %fetch_pages.1), calls=%async_computation | async-start | bytes 4194304 | tf_op jit(solution)/shard_map/all_to_all | solution.py:342
  20.8 0.8 exponential_multiply_fusion
  22.3 1.3 copy.29
  23.6 1.4 copy.30
  27.3 25.0 %block_work.1 = (f32[256,8192]{1,0:T(8,128)}, bf16[8192,128]{1,0:T(8,128)(2,1)}, bf16[256,1024]{1,0:T(8,128)(2,1)}) custom-call(bf16[1,256,10240]{2,1,0:T(8,128)(2,1)} %cin.1, bf16[1,256,10240]{2,1,0:T(8,128)(2,1)} %cin.1, bf16[1,256,10240]{2,1,0:T(8,128)(2,1)} %cin.1, f32[8,10240]{1,0:T(8,128)} %pad_convert_fusion.rimx.rimb.rimc, ...), custom_call_target="tpu_custom_call" | custom-call | flops 1000 | bytes 1000 | tf_op jit(solution)/shard_map/block_work/pallas_call | solution.py:141
  52.4 3.0 %fusion.16 = (bf16[4096,128]{1,0:T(8,128)(2,1)}, bf16[4096,128]{1,0:T(8,128)(2,1)}) fusion(bf16[8192,128]{1,0:T(8,128)(2,1)} %get-tuple-element.14.a, s32[]{:T(128)S(6)} %select_n.121), kind=kLoop, calls=%fused_computation.58 | loop fusion | bytes 4194308 | tf_op jit(solution)/shard_map/slice | solution.py:398
  59.4 3.2 %collective-permute-start.4 = (bf16[4096,128]{1,0:T(8,128)(2,1)}, bf16[4096,128]{1,0:T(8,128)(2,1)}, u32[]{:S(2)}, u32[]{:S(2)}) collective-permute-start(bf16[4096,128]{1,0:T(8,128)(2,1)} %get-tuple-element.21), channel_id=1, source_target_pairs={{0,1},{2,3},{4,5},{6,7},{8,9},{10,11},{12,13},{14,15},{16,17},{18,... | collective-permute-start | bytes 3145736 | tf_op jit(solution)/shard_map/ppermute | solution.py:398
  62.7 7.0 %all-to-all-done.old = bf16[32,256,128]{2,1,0:T(8,128)(2,1)S(1)} async-done(((bf16[32,256,128]{2,1,0:T(8,128)(2,1)}), bf16[32,256,128]{2,1,0:T(8,128)(2,1)S(1)}, u32[]{:S(2)}, u32[]{:S(2)}) %all-to-all-start) | async-done | bytes 2097184 | tf_op jit(solution)/shard_map/all_to_all | solution.py:342
  69.7 1.6 %copy-done = bf16[8192,128]{1,0:T(8,128)(2,1)S(1)} copy-done((bf16[8192,128]{1,0:T(8,128)(2,1)S(1)}, bf16[8192,128]{1,0:T(8,128)(2,1)}, u32[]{:S(2)}) %copy-start) | copy-done | bytes 2097176
  71.3 2.0 %combine.1 = bf16[32,256,128]{2,1,0:T(8,128)(2,1)S(1)} custom-call(s32[32]{0:T(128)S(1)} %select_reduce_fusion.1.pages, f32[64]{0:T(128)S(1)} %get-tuple-element.33.scale_a, f32[64]{0:T(128)S(1)} %get-tuple-element.32.scale_b, f32[64]{0:T(128)S(1)} %dynamic_slice.22.scale_old, s32[1]{0:T(128)} %bitcast.17.which, bf16[8192,128]{1,0:T(8,128)(2,1)S(1)} %copy-done, ...), custom_call_target="tpu_custom_call" | custom-call | bytes 6291456 | tf_op jit(solution)/shard_map/combine/pallas_call | solution.py:241
  73.3 1.3 copy-done.1
  74.7 3.8 %gather_fusion.1 = bf16[3,10240]{1,0:T(4,128)(2,1)S(1)} fusion(bf16[256,10240]{1,0:T(8,128)(2,1)} %bitcast.61, s32[1024]{0:T(1024)S(1)} %pad_clamp_fusion), kind=kCustom, calls=%fused_computation.1 | custom fusion | bytes 122892 | tf_op jit(solution)/shard_map/gather | solution.py:416
  78.7 1.0 broadcast_select_fusion
  81.1 4.2 %all-to-all-start.1 = ((bf16[32,256,128]{2,1,0:T(8,128)(2,1)}), bf16[32,256,128]{2,1,0:T(8,128)(2,1)S(1)}, u32[]{:S(2)}, u32[]{:S(2)}) async-start(bf16[32,256,128]{2,1,0:T(8,128)(2,1)} %copy-done.1), calls=%async_computation.1 | async-start | bytes 4194304 | tf_op jit(solution)/shard_map/all_to_all | solution.py:396
  86.0 1.4 broadcast_select_fusion.2
  87.4 13.1 %add_convert_fusion.rst = bf16[8192,128]{1,0:T(8,128)(2,1)} fusion(bf16[4096,128]{1,0:T(8,128)(2,1)S(1)} %get-tuple-element.24, bf16[4096,128]{1,0:T(8,128)(2,1)S(1)} %get-tuple-element.23, bf16[4096,128]{1,0:T(8,128)(2,1)S(1)} %copy-done.3, bf16[4096,128]{1,0:T(8,128)(2,1)} %collective-permute-done.4, f32[8192]{0:T(1024)S(1)} %mul.74), kind=kLoop, calls=%fused_computation.2 | loop fusion | flops 11534336 | bytes 6324224 | tf_op jit(solution)/shard_map/convert_element_type | solution.py:409
  100.5 12.5 %finish.1.after = bf16[1,256,8192]{2,1,0:T(8,128)(2,1)} custom-call(s32[1]{0:T(128)} %bitcast.1.count, f32[256,8192]{1,0:T(8,128)} %get-tuple-element.12.y, bf16[256,1024]{1,0:T(8,128)(2,1)} %get-tuple-element.13.c, bf16[8192,128]{1,0:T(8,128)(2,1)} %add_convert_fusion.rst, f32[8,256,16]{2,1,0:T(8,128)} %bitcast.63, bf16[1,256,8192]{2,1,0:T(8,128)(2,1)} %gate.1, ...), custom_call_target="tpu_custom_call" | custom-call | flops 1000 | bytes 1000 | tf_op jit(solution)/shard_map/finish/pallas_call | solution.py:194
  113.0 21.0 %all-to-all-done.1.back = bf16[32,256,128]{2,1,0:T(8,128)(2,1)S(1)} async-done(((bf16[32,256,128]{2,1,0:T(8,128)(2,1)}), bf16[32,256,128]{2,1,0:T(8,128)(2,1)S(1)}, u32[]{:S(2)}, u32[]{:S(2)}) %all-to-all-start.1) | async-done | bytes 2097184 | tf_op jit(solution)/shard_map/all_to_all | solution.py:396
  134.0 1.4 copy-done.2
  135.4 6.4 %store_pages.1 = f32[32,256,128]{2,1,0:T(8,128)} custom-call(s32[32]{0:T(128)} %select_reduce_fusion.source, s32[32]{0:T(128)} %convert_element_type.46.used, f32[32,256,128]{2,1,0:T(8,128)} %pool.3, bf16[32,256,128]{2,1,0:T(8,128)(2,1)} %copy-done.2, bf16[1,256,8192]{2,1,0:T(8,128)(2,1)} %finish.1.after), custom_call_target="tpu_custom_call" | custom-call | bytes 10485760 | tf_op jit(solution)/shard_map/store_pages/pallas_call | solution.py:279
  (78 shorter events, 10.5 us)
Async XLA Ops:
  0.6 11.0 %copy-start.10 = (f32[128]{0:T(128)S(1)}, f32[128]{0:T(128)}, u32[]{:S(2)}) copy-start(f32[128]{0:T(128)} %param.21) | copy-start | bytes 1540
  0.6 11.0 %copy-start.6 = (bf16[1,256,128]{2,1,0:T(8,128)(2,1)S(1)}, bf16[1,256,128]{2,1,0:T(8,128)(2,1)}, u32[]{:S(2)}) copy-start(bf16[1,256,128]{2,1,0:T(8,128)(2,1)} %param.17) | copy-start | bytes 196612
  0.7 11.1 %copy-start.11 = (s32[16]{0:T(128)S(1)}, s32[16]{0:T(128)}, u32[]{:S(2)}) copy-start(s32[16]{0:T(128)} %param.29) | copy-start | bytes 196
  0.7 12.4 %copy-start.7 = (f32[128]{0:T(128)S(1)}, f32[128]{0:T(128)}, u32[]{:S(2)}) copy-start(f32[128]{0:T(128)} %param.20) | copy-start | bytes 1540
  9.2 12.4 %copy-start.12 = (s32[16]{0:T(128)S(1)}, s32[16]{0:T(128)}, u32[]{:S(2)}) copy-start(s32[16]{0:T(128)} %param.28) | copy-start | bytes 196
  9.2 17.2 %collective-permute-start = (bf16[3,10240]{1,0:T(4,128)(2,1)S(1)}, bf16[3,10240]{1,0:T(4,128)(2,1)S(1)}, u32[]{:S(2)}, u32[]{:S(2)}) collective-permute-start(bf16[3,10240]{1,0:T(4,128)(2,1)S(1)} %slice_bitcast_fusion), channel_id=1, source_target_pairs={{0,1},{2,3},{4,5},{6,7},{8,9},{10,11},{12,13},{14,15},{16,17},{18,... | collective-permute-start | bytes 184328 | tf_op jit(solution)/shard_map/ppermute | solution.py:345
  13.3 11.6 %copy-start.9 = (f32[128]{0:T(128)S(1)}, f32[128]{0:T(128)}, u32[]{:S(2)}) copy-start(f32[128]{0:T(128)} %param.22) | copy-start | bytes 1540
  13.5 13.0 %copy-start.5 = (bf16[1,3,10240]{2,1,0:T(4,128)(2,1)S(1)}, bf16[1,3,10240]{2,1,0:T(4,128)(2,1)}, u32[]{:S(2)}) copy-start(bf16[1,3,10240]{2,1,0:T(4,128)(2,1)} %param.24) | copy-start | bytes 184324
  13.8 13.5 %copy-start.4 = (f32[16,8,2,128]{3,1,2,0:T(8,128)}, f32[16,8,2,128]{3,1,2,0:T(8,128)S(1)}, u32[]{:S(2)}) copy-start(f32[16,8,2,128]{3,1,2,0:T(8,128)S(1)} %copy.37) | copy-start | bytes 393220
  14.0 45.1 %collective-permute-start.1 = (f32[128]{0:T(128)S(1)}, f32[128]{0:T(128)S(1)}, u32[]{:S(2)}, u32[]{:S(2)}) collective-permute-start(f32[128]{0:T(128)S(1)} %exp.16), channel_id=1, source_target_pairs={{0,1},{1,0},{2,3},{3,2},{4,5},{5,4},{6,7},{7,6},{8,9},{9,8},{10,11... | collective-permute-start | bytes 1544 | tf_op jit(solution)/shard_map/ppermute | solution.py:357
  14.1 55.6 %all-to-all-start = ((bf16[32,256,128]{2,1,0:T(8,128)(2,1)}), bf16[32,256,128]{2,1,0:T(8,128)(2,1)S(1)}, u32[]{:S(2)}, u32[]{:S(2)}) async-start(bf16[32,256,128]{2,1,0:T(8,128)(2,1)} %fetch_pages.1), calls=%async_computation | async-start | bytes 4194304 | tf_op jit(solution)/shard_map/all_to_all | solution.py:342
  52.4 4.7 %copy-start.8 = (s32[32]{0:T(128)S(1)}, s32[32]{0:T(128)}, u32[]{:S(2)}) copy-start(s32[32]{0:T(128)} %select_reduce_fusion.2.slots) | copy-start | bytes 388
  55.4 7.2 %collective-permute-start.2 = (bf16[4096,128]{1,0:T(8,128)(2,1)}, bf16[4096,128]{1,0:T(8,128)(2,1)S(1)}, u32[]{:S(2)}, u32[]{:S(2)}) collective-permute-start(bf16[4096,128]{1,0:T(8,128)(2,1)} %get-tuple-element.22), channel_id=1, source_target_pairs={{0,1},{1,0},{2,3},{3,2},{4,5},{5,4},{6,7},{7,6},{8,9},{9,8},{10,11... | collective-permute-start | bytes 3145736 | tf_op jit(solution)/shard_map/ppermute | solution.py:375
  59.4 28.0 %collective-permute-start.4 = (bf16[4096,128]{1,0:T(8,128)(2,1)}, bf16[4096,128]{1,0:T(8,128)(2,1)}, u32[]{:S(2)}, u32[]{:S(2)}) collective-permute-start(bf16[4096,128]{1,0:T(8,128)(2,1)} %get-tuple-element.21), channel_id=1, source_target_pairs={{0,1},{2,3},{4,5},{6,7},{8,9},{10,11},{12,13},{14,15},{16,17},{18,... | collective-permute-start | bytes 3145736 | tf_op jit(solution)/shard_map/ppermute | solution.py:398
  69.7 1.6 %copy-start = (bf16[8192,128]{1,0:T(8,128)(2,1)S(1)}, bf16[8192,128]{1,0:T(8,128)(2,1)}, u32[]{:S(2)}) copy-start(bf16[8192,128]{1,0:T(8,128)(2,1)} %get-tuple-element.14.a) | copy-start | bytes 6291460
  73.3 1.4 copy-start.1
  78.6 6.7 %collective-permute-start.5 = (bf16[3,10240]{1,0:T(4,128)(2,1)S(1)}, bf16[3,10240]{1,0:T(4,128)(2,1)S(1)}, u32[]{:S(2)}, u32[]{:S(2)}) collective-permute-start(bf16[3,10240]{1,0:T(4,128)(2,1)S(1)} %broadcast_select_fusion.3), channel_id=1, source_target_pairs={{0,1},{1,0},{2,3},{3,2},{4,5},{5,4},{6,7},{7,6},{8,9},{9,8},{10,11... | collective-permute-start | bytes 184328 | tf_op jit(solution)/shard_map/ppermute | solution.py:417
  80.5 5.5 %collective-permute-start.3 = (bf16[4096,128]{1,0:T(8,128)(2,1)S(1)}, bf16[4096,128]{1,0:T(8,128)(2,1)}, u32[]{:S(2)}, u32[]{:S(2)}) collective-permute-start(bf16[4096,128]{1,0:T(8,128)(2,1)S(1)} %bitcast.64), channel_id=1, source_target_pairs={{0,1},{1,0},{2,3},{3,2},{4,5},{5,4},{6,7},{7,6},{8,9},{9,8},{10,11... | collective-permute-start | bytes 3145736 | tf_op jit(solution)/shard_map/ppermute | solution.py:401
  81.1 53.0 %all-to-all-start.1 = ((bf16[32,256,128]{2,1,0:T(8,128)(2,1)}), bf16[32,256,128]{2,1,0:T(8,128)(2,1)S(1)}, u32[]{:S(2)}, u32[]{:S(2)}) async-start(bf16[32,256,128]{2,1,0:T(8,128)(2,1)} %copy-done.1), calls=%async_computation.1 | async-start | bytes 4194304 | tf_op jit(solution)/shard_map/all_to_all | solution.py:396
  85.3 2.2 %copy-start.3 = (bf16[4096,128]{1,0:T(8,128)(2,1)S(1)}, bf16[4096,128]{1,0:T(8,128)(2,1)}, u32[]{:S(2)}) copy-start(bf16[4096,128]{1,0:T(8,128)(2,1)} %broadcast_select_fusion) | copy-start | bytes 3145732
  134.0 1.4 copy-start.2
